TPU v7x, 256 devices: a whole 4x4x8 slice. The times are simulated.
256 devices in a mesh: row: 8 (over x, y_hi), col: 32 (over z, y_lo, core).
Axes of the slice: x: 4, y: 4 (y_hi: 2, y_lo: 2; y = y_hi * 2 + y_lo), z: 8, core: 2. Of those that a mesh axis runs over, the one named last changes fastest.
Arguments:
- position: float32 [3, 1048576], P(None, ('row', 'col')), may hold values from -6 to 6
- velocity: float32 [3, 1048576], P(None, ('row', 'col')), may hold values from -4 to 4
- accel_old: float32 [3, 1048576], P(None, ('row', 'col')), may hold values from -6 to 6
- jerk_old: float32 [3, 1048576], P(None, ('row', 'col')), may hold values from -12 to 12
- mass: float32 [1048576], P(('row', 'col')), may hold values from 4.7683716e-07 to 4.7683716e-06
- elapsed: float32 [1048576], P(('row', 'col')), may hold values from 0.05 to 0.5
- active_index: int32 [2048], P(('row', 'col')), may hold values from 0 to 4095, as said below
- active_count: int32 [256], P(('row', 'col')), may hold values from 1 to 8, as said below
Outputs:
- accel_new: float32 [3, 2048], P(None, ('row', 'col'))
- jerk_new: float32 [3, 2048], P(None, ('row', 'col'))
Inputs may be any that keep to these rules, and one draw needn't show every extreme that they name: `active_index`: within each device's 8 slots the entries are distinct indices into that device's 4096 stars; entries of slots that are not live are ignored. `active_count`: most devices have few live slots; some device fills all of them.
All inputs are finite; a program needn't handle non-finite values.
Results may differ from a plain program's by a relative error of at most 0.0003.
Values sent between devices are 32-bit elements; how exact they have to be, the bound alone decides.
A program may use at most 64 MiB of HBM per device.

v0:
```python
import math

import jax
import jax.numpy as jnp
from jax import lax
from jax.sharding import PartitionSpec as P

SOFTENING = 0.0025


def predict(position, velocity, accel_old, jerk_old, elapsed):
    step_dt = elapsed[None, :]
    pos_pred = position + step_dt * (
        velocity + step_dt * (0.5 * accel_old + step_dt * (jerk_old / 6.0))
    )
    vel_pred = velocity + step_dt * (accel_old + step_dt * (0.5 * jerk_old))
    return (pos_pred, vel_pred)


def pair_terms(targets, sources):
    delta_x = sources[0:3, None, :] - targets[0:3, :, None]
    delta_v = sources[3:6, None, :] - targets[3:6, :, None]
    dist_sq = SOFTENING + jnp.sum(delta_x * delta_x, axis=0)
    inv_dist = lax.rsqrt(dist_sq)
    mass_r3 = sources[6][None, :] * inv_dist * inv_dist * inv_dist
    radial = 3.0 * jnp.sum(delta_x * delta_v, axis=0) / dist_sq
    accel_sum = jnp.sum(mass_r3[None] * delta_x, axis=2)
    jerk_sum = jnp.sum(mass_r3[None] * (delta_v - radial[None] * delta_x), axis=2)
    return jnp.concatenate([accel_sum, jerk_sum], axis=0)


def block_terms(targets, sources):
    source_total = sources.shape[1]
    block_width = math.gcd(source_total, 2048)
    blocks = source_total // block_width

    def advance(index, running):
        segment = lax.dynamic_slice_in_dim(sources, index * block_width, block_width, 1)
        return running + pair_terms(targets, segment)

    return lax.fori_loop(0, blocks, advance, jnp.zeros((6, targets.shape[1]), jnp.float32))


def tile_width(slots):
    return min(slots, 512)


def add_forces(running, targets, live_tiles, sources):
    return jnp.where(live_tiles > 0, block_terms(targets, sources), running)


def live_slots(counts, per_owner, slots):
    slot_ids = jnp.arange(slots, dtype=jnp.int32)
    owner_ids = slot_ids // per_owner
    owners = jnp.arange(counts.shape[0], dtype=jnp.int32)
    limit = jnp.sum(jnp.where(owner_ids[:, None] == owners[None, :], counts[None, :], 0), axis=1)
    return slot_ids % per_owner < limit


def arrange(targets):
    slots = targets.shape[1]
    tile_rows = tile_width(slots)
    return (targets, slots // tile_rows, None)


def restore(forces, live_mask):
    return jnp.where(live_mask[None, :], forces, 0.0)


def local(position, velocity, accel_old, jerk_old, mass, elapsed, active_index, active_count):
    pos_pred, vel_pred = predict(position, velocity, accel_old, jerk_old, elapsed)
    packed = jnp.concatenate([pos_pred, vel_pred, mass[None, :]], axis=0)
    own_targets = jnp.take(packed[0:6], active_index, axis=1)
    per_owner = own_targets.shape[1]
    targets, counts = (
        lax.all_gather(own_targets, "row", axis=1, tiled=True),
        lax.all_gather(active_count, "row", axis=0, tiled=True),
    )
    live_mask = live_slots(counts, per_owner, targets.shape[1])
    packed_targets, live_tiles, dense_rank = arrange(targets)
    initial = jnp.zeros(packed_targets.shape, jnp.float32)
    running = add_forces(
        initial, packed_targets, live_tiles, lax.all_gather(packed, "col", axis=1, tiled=True)
    )
    forces = restore(running, live_mask)
    summed = lax.psum_scatter(forces, "row", scatter_dimension=1, tiled=True)
    return (summed[0:3], summed[3:6])


def solution(mesh):
    placed = (
        P(None, ("row", "col")),
        P(None, ("row", "col")),
        P(None, ("row", "col")),
        P(None, ("row", "col")),
        P(("row", "col")),
        P(("row", "col")),
        P(("row", "col")),
        P(("row", "col")),
    )
    return jax.shard_map(
        local,
        mesh=mesh,
        in_specs=placed,
        out_specs=(P(None, ("row", "col")), P(None, ("row", "col"))),
        check_vma=False,
    )
```

profile of v0, /device:TPU:64, one launch (start us, length us, event | category | flops | bytes accessed | tf_op | source)
XLA Modules:
  0.0 320.2 jit_solution(4021482488928725659)
XLA Ops:
  8.9 1.4 pad_maximum_fusion
  11.0 1.3 fusion.9
  13.1 13.2 %all-reduce = s32[8]{0:T(128)S(1)} all-reduce(s32[8]{0:T(128)S(1)} %dynamic-update-slice), channel_id=1, replica_groups=mesh['row'=8,'col'=32] {'row'}, use_global_device_ids=true, to_apply=%add | all-reduce | flops 8 | bytes 64
  27.7 34.1 %all_gather.11 = f32[6,64]{0,1:T(8,128)S(1)} all-gather(f32[6,8]{0,1:T(8,128)S(1)} %select_bitcast_fusion), channel_id=1, replica_groups=mesh['row'=8,'col'=32] {'row'}, dimensions={1}, use_global_device_ids=true | all-gather | bytes 1728 | tf_op jit(solution)/shard_map/all_gather | solution.py:76
  62.6 16.2 %all-gather.2.cloned.1.call-done = f32[7,131072]{1,0:T(8,128)} async-done(((f32[7,4096]{1,0:T(8,128)}), f32[7,131072]{1,0:T(8,128)}) %all-gather.2.cloned.1.call-update) | async-done | bytes 3670032 | tf_op jit(solution)/shard_map/all_gather | solution.py:83
  78.8 209.5 %while.14 = (s32[]{:T(128)}, f32[6,64]{1,0:T(8,128)S(1)}, f32[7,131072]{1,0:T(8,128)}, f32[6,64]{1,0:T(8,128)S(1)}, s32[]{:T(128)}, /*index=5*/s32[]{:T(128)}, s32[]{}, s32[]{:T(128)}, s32[]{:T(128)}, s32[]{}) while((s32[]{:T(128)}, f32[6,64]{1,0:T(8,128)S(1)}, f32[7,131072]{1,0:T(8,128)}, f32[6,64]{1,0:T(8,128)S(1)}, s32[]{:T(128)}, ...), condition=%wide.region_6.7_spmd.clone, body=%wide.region_1.6_spmd.clone.sunk | while | flops 6030089 | bytes 4427969 | solution.py:41
  82.1 1.0 fusion.15
  88.6 1.0 fusion.15
  95.2 1.0 fusion.15
  101.7 1.0 fusion.15
  108.3 1.0 fusion.15
  114.8 1.0 fusion.15
  121.4 1.0 fusion.15
  124.6 1.0 fusion.15
  127.9 1.0 fusion.15
  131.2 1.0 fusion.15
  137.7 1.0 fusion.15
  144.3 1.0 fusion.15
  150.8 1.0 fusion.15
  157.4 1.0 fusion.15
  163.9 1.0 fusion.15
  170.5 1.0 fusion.15
  177.0 1.0 fusion.15
  183.6 1.0 fusion.15
  186.9 1.0 fusion.15
  190.1 1.0 fusion.15
  193.4 1.0 fusion.15
  200.0 1.0 fusion.15
  206.5 1.0 fusion.15
  213.0 1.0 fusion.15
  219.6 1.0 fusion.15
  288.4 24.3 %all-reduce.1 = f32[6,64]{1,0:T(8,128)S(1)} all-reduce(f32[6,64]{1,0:T(8,128)S(1)} %broadcast_select_fusion), channel_id=2, replica_groups=mesh['row'=8,'col'=32] {'row'}, use_global_device_ids=true, to_apply=%region_7.8.clone | all-reduce | flops 384 | bytes 3072
  (446 shorter events, 186.5 us)
Async XLA Ops:
  7.2 71.6 %all-gather.2.cloned.1.call-start = ((), (), s32[]{:S(2)}) async-start(), calls=%async_computation | async-start | bytes 4325376 | tf_op jit(solution)/shard_map/all_gather | solution.py:83
  8.9 18.0 %copy-start = (s32[8]{0:T(128)S(1)}, s32[8]{0:T(128)}, u32[]{:S(2)}) copy-start(s32[8]{0:T(128)} %param.16) | copy-start | bytes 100
Sparse Core Ops, SparseCore 0:
  10.5 68.2 all-gather.1
where the time goes:
time: 327 us; the launch traced here: 320 us
  local copies, waits for them, and re-layouts  128 us (39%)
  other arithmetic  86.5 us (26%)
  blocking collectives  71.6 us (22%)
  waiting for transfers between devices  16.2 us (5%)
  between operations  15.4 us (5%)
    slice x128, local copies, waits for them, and re-layouts, pair_terms(): delta_v = sources[3:6, None, :] - targets[3:6, :, None]  64.4 us
    slice x64, local copies, waits for them, and re-layouts, pair_terms(): mass_r3 = sources[6][None, :] * inv_dist * inv_dist * inv_dist  59.4 us
    reduce_sum x64, other arithmetic, pair_terms(): accel_sum = jnp.sum(mass_r3[None] * delta_x, axis=2)  44.5 us
    unnamed x2, blocking collectives  37.5 us
    all_gather x1, blocking collectives, local(): lax.all_gather(own_targets, 'row', axis=1, tiled=True)  34.1 us
    reduce_sum x64, other arithmetic, pair_terms(): dist_sq = SOFTENING + jnp.sum(delta_x * delta_x, axis=0)  28.3 us
    all_gather x1, waiting for transfers between devices, local(): lax.all_gather(packed, 'col', axis=1, tiled=True)  16.2 us
    div x64, other arithmetic, pair_terms(): radial = 3.0 * jnp.sum(delta_x * delta_v, axis=0) / dist_sq  9.53 us
  transfers between devices with their start and end apart: 1, of which 1 were waited for; matrix products, arithmetic and copies ran while one was open for 1% of the time, Pallas kernels for 0%

commit v1 on v0

v1 whole, which is shorter than its diff:
```python
import functools

import jax
import jax.numpy as jnp
from jax import lax
from jax.experimental import pallas as pl
from jax.experimental.pallas import tpu as pltpu
from jax.sharding import PartitionSpec as P

SOFTENING = 0.0025
MESH = pl.DeviceIdType.MESH
LANES = 128
GROUP = 16
DEVICES = GROUP * GROUP
SLOT_LANES = 16
ACT = 8
STARS = 4096
TILES = STARS // LANES
SLOTS = DEVICES * ACT
ROWS = SLOTS + 16


def place():
    row = lax.axis_index("row")
    col = lax.axis_index("col")
    core = lax.rem(col, 2)
    return row, col, core, lax.div(col, 2), row * 2 + core


def zy_peer(step):
    row, col, core, zy, rc = place()
    peer = lax.rem(zy + step, GROUP)
    return peer, (row, peer * 2 + core)


def rc_peer(step):
    row, col, core, zy, rc = place()
    peer = lax.rem(rc + step, GROUP)
    return peer, (lax.div(peer, 2), zy * 2 + lax.rem(peer, 2))


def greet():
    barrier = pltpu.get_barrier_semaphore()
    for step in range(1, GROUP):
        for peer in (zy_peer, rc_peer):
            pl.semaphore_signal(barrier, inc=1, device_id=peer(step)[1], device_id_type=MESH)


def await_greetings():
    pl.semaphore_wait(pltpu.get_barrier_semaphore(), 2 * (GROUP - 1))


def wait_bytes(ref, sem):
    pltpu.make_async_copy(ref, ref, sem).wait()


def gather_kernel(index_ref, count_ref, pos_ref, vel_ref, acc_ref, jerk_ref, elapsed_ref,
                  p_ref, v_ref, all_ref, offset_ref, mine, send_sem, recv_sem):
    row, col, core, zy, rc = place()
    greet()
    for tile in range(TILES):
        cols = pl.ds(tile * LANES, LANES)
        dt = elapsed_ref[tile:tile + 1, :]
        vel, acc, jerk = vel_ref[:, cols], acc_ref[:, cols], jerk_ref[:, cols]
        p_ref[:, cols] = pos_ref[:, cols] + dt * (vel + dt * (0.5 * acc + dt * (jerk * (1.0 / 6.0))))
        v_ref[:, cols] = vel + dt * (acc + dt * (0.5 * jerk))
    lane = lax.broadcasted_iota(jnp.int32, (3, LANES), 1)
    sub = lax.broadcasted_iota(jnp.int32, (3, LANES), 0)
    total = jnp.zeros((3, LANES), jnp.float32)
    for slot in range(ACT):
        away = lane - index_ref[slot]
        picked = [jnp.zeros((3, LANES), jnp.float32)] * 2
        for tile in range(TILES):
            cols = pl.ds(tile * LANES, LANES)
            hit = away == -tile * LANES
            picked = [jnp.where(hit, ref[:, cols], old) for ref, old in zip((p_ref, v_ref), picked)]
        for first, value in zip((0, 3), picked):
            value = jnp.sum(value, axis=1, keepdims=True)
            lead = (ACT - slot) % ACT * SLOT_LANES + first
            total = total + jnp.where(lane == sub + lead, value, 0.0)
    packed = jnp.sum(total, axis=0, keepdims=True)
    count = count_ref[0].astype(jnp.float32)
    packed = jnp.where(lane[0:1] == 6, count, packed)
    mine[...] = packed
    me = rc * GROUP + zy
    all_ref[pl.ds(me, 1), :] = packed
    await_greetings()
    for step in range(1, GROUP):
        peer, device = zy_peer(step)
        pltpu.make_async_remote_copy(
            src_ref=mine, dst_ref=all_ref.at[pl.ds(me, 1)],
            send_sem=send_sem.at[0], recv_sem=recv_sem.at[0],
            device_id=device, device_id_type=MESH).start()
    wait_bytes(all_ref.at[pl.ds(0, GROUP - 1)], recv_sem.at[0])
    block = all_ref.at[pl.ds(pl.multiple_of(rc * GROUP, GROUP), GROUP)]
    for step in range(1, GROUP):
        peer, device = rc_peer(step)
        pltpu.make_async_remote_copy(
            src_ref=block, dst_ref=block,
            send_sem=send_sem.at[1], recv_sem=recv_sem.at[1],
            device_id=device, device_id_type=MESH).start()
    wait_bytes(all_ref.at[pl.ds(0, GROUP - 1)], send_sem.at[0])
    wait_bytes(all_ref.at[pl.ds(0, (GROUP - 1) * GROUP)], recv_sem.at[1])
    counts = all_ref[...].astype(jnp.bfloat16)
    before = lax.broadcasted_iota(jnp.int32, (DEVICES, DEVICES), 0)
    after = lax.broadcasted_iota(jnp.int32, (DEVICES, DEVICES), 1)
    ahead = jnp.where(before < after, 1.0, 0.0).astype(jnp.bfloat16)
    whole = jnp.where(before >= 0, 1.0, 0.0).astype(jnp.bfloat16)
    column = lax.broadcasted_iota(jnp.int32, (DEVICES, LANES), 1)
    counts = jnp.where(column == 6, all_ref[...], 0.0).astype(jnp.bfloat16)
    dims = (((0,), (0,)), ((), ()))
    starts = lax.dot_general(counts, ahead, dims, preferred_element_type=jnp.float32)
    totals = lax.dot_general(counts, whole, dims, preferred_element_type=jnp.float32)
    offset_ref[0:1, :] = starts[6:7, :].astype(jnp.int32)
    offset_ref[1:2, :] = totals[6:7, :].astype(jnp.int32)
    wait_bytes(all_ref.at[pl.ds(0, (GROUP - 1) * GROUP)], send_sem.at[1])


def force_kernel(offset_ref, p_ref, v_ref, mass_ref, all_ref, out_ref, targets, results):
    live = offset_ref[1, 0]
    targets[...] = jnp.zeros_like(targets)

    def pack(device, carry):
        spread = jnp.broadcast_to(all_ref[pl.ds(device, 1), :], (ACT, LANES))
        spread = pltpu.roll(spread, 0, 1, stride=SLOT_LANES, stride_axis=0)
        targets[pl.ds(offset_ref[0, device], ACT), :] = spread
        return carry

    lax.fori_loop(0, DEVICES, pack, 0, unroll=8)
    lane = lax.broadcasted_iota(jnp.int32, (ACT, LANES), 1)

    def group(index, carry):
        rows = pl.ds(pl.multiple_of(index * ACT, ACT), ACT)
        block = targets[rows, :]
        mine = [jnp.broadcast_to(block[:, f:f + 1], (ACT, LANES)) for f in range(6)]
        sums = [jnp.zeros((ACT, LANES), jnp.float32) for _ in range(9)]
        for tile in range(TILES):
            cols = pl.ds(tile * LANES, LANES)
            dx = [p_ref[f:f + 1, cols] - mine[f] for f in range(3)]
            dv = [v_ref[f:f + 1, cols] - mine[3 + f] for f in range(3)]
            r2 = dx[0] * dx[0] + dx[1] * dx[1] + dx[2] * dx[2] + SOFTENING
            dot = dx[0] * dv[0] + dx[1] * dv[1] + dx[2] * dv[2]
            inv = lax.rsqrt(r2)
            inv2 = inv * inv
            w = mass_ref[tile:tile + 1, :] * inv * inv2
            u = w * (dot * inv2)
            for f in range(3):
                sums[f] = sums[f] + w * dx[f]
                sums[3 + f] = sums[3 + f] + w * dv[f]
                sums[6 + f] = sums[6 + f] + u * dx[f]
        value = jnp.zeros((ACT, LANES), jnp.float32)
        for f in range(3):
            value = jnp.where(lane == f, jnp.sum(sums[f], axis=1, keepdims=True), value)
            both = sums[3 + f] - 3.0 * sums[6 + f]
            value = jnp.where(lane == 3 + f, jnp.sum(both, axis=1, keepdims=True), value)
        results[rows, :] = value
        return carry

    lax.fori_loop(0, lax.div(live + (ACT - 1), ACT), group, 0)
    slot = lax.broadcasted_iota(jnp.int32, (ACT, LANES), 0)
    own = lax.div(lane, SLOT_LANES) == slot

    def unpack(device, carry):
        block = results[pl.ds(offset_ref[0, device], ACT), :]
        block = pltpu.roll(block, 0, 1, stride=SLOT_LANES, stride_axis=0)
        out_ref[pl.ds(device, 1), :] = jnp.sum(jnp.where(own, block, 0.0), axis=0, keepdims=True)
        return carry

    lax.fori_loop(0, DEVICES, unpack, 0, unroll=8)


def scatter_kernel(count_ref, part_ref, accel_ref, jerk_ref, first, second, summed, send_sem, recv_sem):
    row, col, core, zy, rc = place()
    greet()
    await_greetings()
    for step in range(1, GROUP):
        peer, device = rc_peer(step)
        pltpu.make_async_remote_copy(
            src_ref=part_ref.at[pl.ds(pl.multiple_of(peer * GROUP, GROUP), GROUP)],
            dst_ref=first.at[step - 1],
            send_sem=send_sem.at[0], recv_sem=recv_sem.at[0],
            device_id=device, device_id_type=MESH).start()
    total = part_ref[pl.ds(pl.multiple_of(rc * GROUP, GROUP), GROUP), :]
    wait_bytes(first, recv_sem.at[0])
    for step in range(1, GROUP):
        total = total + first[step - 1]
    summed[...] = total
    for step in range(1, GROUP):
        peer, device = zy_peer(step)
        pltpu.make_async_remote_copy(
            src_ref=summed.at[pl.ds(peer, 1)],
            dst_ref=second.at[pl.ds(step - 1, 1)],
            send_sem=send_sem.at[1], recv_sem=recv_sem.at[1],
            device_id=device, device_id_type=MESH).start()
    final = summed[pl.ds(zy, 1), :]
    wait_bytes(second.at[pl.ds(0, GROUP - 1)], recv_sem.at[1])
    final = final + jnp.sum(second[0:GROUP - 1, :], axis=0, keepdims=True)
    sub = lax.broadcasted_iota(jnp.int32, (8, LANES), 0)
    lane = lax.broadcasted_iota(jnp.int32, (8, LANES), 1)
    spread = jnp.where(lax.rem(lane, SLOT_LANES) == sub, jnp.broadcast_to(final, (8, LANES)), 0.0)
    at = lax.broadcasted_iota(jnp.int32, (8, ACT), 1)
    out = jnp.zeros((8, ACT), jnp.float32)
    for s in range(ACT):
        part = jnp.where(lax.div(lane, SLOT_LANES) == s, spread, 0.0)
        out = jnp.where(at == s, jnp.sum(part, axis=1, keepdims=True), out)
    out = jnp.where(at < count_ref[0], out, 0.0)
    accel_ref[...] = out[0:3]
    jerk_ref[...] = out[3:6]
    wait_bytes(first, send_sem.at[0])
    wait_bytes(second.at[pl.ds(0, GROUP - 1)], send_sem.at[1])


def local(position, velocity, accel_old, jerk_old, mass, elapsed, active_index, active_count):
    f32 = jnp.float32
    vmem = pl.BlockSpec(memory_space=pltpu.VMEM)
    smem = pl.BlockSpec(memory_space=pltpu.SMEM)
    pos, vel, everyone, offsets = pl.pallas_call(
        gather_kernel,
        out_shape=(
            jax.ShapeDtypeStruct((3, STARS), f32),
            jax.ShapeDtypeStruct((3, STARS), f32),
            jax.ShapeDtypeStruct((DEVICES, LANES), f32),
            jax.ShapeDtypeStruct((2, DEVICES), jnp.int32),
        ),
        in_specs=[smem, smem] + [vmem] * 5,
        out_specs=(vmem,) * 4,
        scratch_shapes=[
            pltpu.VMEM((1, LANES), f32),
            pltpu.SemaphoreType.DMA((2,)),
            pltpu.SemaphoreType.DMA((2,)),
        ],
        compiler_params=pltpu.CompilerParams(collective_id=0, has_side_effects=True),
        name="gather_targets",
    )(active_index, active_count, position, velocity, accel_old, jerk_old, elapsed.reshape(TILES, LANES))
    parts = pl.pallas_call(
        force_kernel,
        out_shape=jax.ShapeDtypeStruct((DEVICES, LANES), f32),
        in_specs=[smem] + [vmem] * 4,
        out_specs=vmem,
        scratch_shapes=[pltpu.VMEM((ROWS, LANES), f32), pltpu.VMEM((ROWS, LANES), f32)],
        name="forces",
    )(offsets, pos, vel, mass.reshape(TILES, LANES), everyone)
    return pl.pallas_call(
        scatter_kernel,
        out_shape=(jax.ShapeDtypeStruct((3, ACT), f32), jax.ShapeDtypeStruct((3, ACT), f32)),
        in_specs=[smem, vmem],
        out_specs=(vmem, vmem),
        scratch_shapes=[
            pltpu.VMEM((GROUP - 1, GROUP, LANES), f32),
            pltpu.VMEM((GROUP, LANES), f32),
            pltpu.VMEM((GROUP, LANES), f32),
            pltpu.SemaphoreType.DMA((2,)),
            pltpu.SemaphoreType.DMA((2,)),
        ],
        compiler_params=pltpu.CompilerParams(collective_id=1, has_side_effects=True),
        name="scatter_forces",
    )(active_count, parts)


def solution(mesh):
    split = P(None, ("row", "col"))
    flat = P(("row", "col"))
    return jax.shard_map(
        local,
        mesh=mesh,
        in_specs=(split, split, split, split, flat, flat, flat, flat),
        out_specs=(split, split),
        check_vma=False,
    )
```

time: 327 us -> 77.5 us (0.24)
  the two profiles are of different devices: /device:TPU:64 before, /device:TPU:1 now
where the time goes in v1:
time: 77.5 us; the launch traced here: 77.3 us
  Pallas kernels  74.1 us (96%)
  local copies, waits for them, and re-layouts  1.89 us (2%)
  between operations  1.31 us (2%)
    pallas_call x1, Pallas kernels, local(): pl.pallas_call(force_kernel, out_shape=jax.ShapeDtypeStruct((DEVICES, LAN...  36.6 us
    pallas_call x1, Pallas kernels, local(): pl.pallas_call(gather_kernel, out_shape=(jax.ShapeDtypeStruct((3, STARS),...  22.6 us
    pallas_call x1, Pallas kernels, local(): pl.pallas_call(scatter_kernel, out_shape=(jax.ShapeDtypeStruct((3, ACT),...  14.9 us
    unnamed x6, local copies, waits for them, and re-layouts  1.89 us

profile of v1, /device:TPU:1, one launch (start us, length us, event | category | flops | bytes accessed | tf_op | source)
XLA Modules:
  0.0 77.3 jit_solution(8474527096405006732)
XLA Ops:
  1.3 22.6 %gather_targets.1 = (f32[3,4096]{1,0:T(4,128)}, f32[3,4096]{1,0:T(4,128)}, f32[256,128]{1,0:T(8,128)}, s32[2,256]{1,0:T(2,128)}) custom-call(s32[8]{0:T(128)} %index_ref.1, s32[1]{0:T(128)S(6)} %copy.12.count_ref, f32[3,4096]{1,0:T(4,128)} %pos_ref.1, f32[3,4096]{1,0:T(4,128)} %vel_ref.1, f32[3,4096]{1,0:T(4,128)} %acc_ref.1, f32[3,4096]{1,0:T(4,128)} %jerk_ref.1, ...), custom_call_target="tpu_custom_call" | custom-call | tf_op jit(solution)/shard_map/gather_targets/pallas_call | solution.py:217
  23.9 36.6 %forces.1.part_ref = f32[256,128]{1,0:T(8,128)} custom-call(s32[2,256]{1,0:T(2,128)} %get-tuple-element.6.offset_ref, f32[3,4096]{1,0:T(4,128)} %get-tuple-element.7.p_ref, f32[3,4096]{1,0:T(4,128)} %get-tuple-element.8.v_ref, f32[32,128]{1,0:T(8,128)} %bitcast.3, f32[256,128]{1,0:T(8,128)} %get-tuple-element.9.all_ref), custom_call_target="tpu_custom_call" | custom-call | tf_op jit(solution)/shard_map/forces/pallas_call | solution.py:235
  60.5 14.9 %scatter_forces.1 = (f32[3,8]{1,0:T(4,128)}, f32[3,8]{1,0:T(4,128)}) custom-call(s32[1]{0:T(128)S(6)} %copy.12.count_ref, f32[256,128]{1,0:T(8,128)} %forces.1.part_ref), custom_call_target="tpu_custom_call" | custom-call | tf_op jit(solution)/shard_map/scatter_forces/pallas_call | solution.py:243
  75.4 0.0 copy-start.1
  75.4 0.7 copy-done.1
  76.1 0.0 copy-start
  76.1 0.6 copy.13
  76.7 0.1 copy-done
  76.7 0.6 copy.14
Async XLA Ops:
  75.4 0.7 copy-start.1
  76.1 0.7 copy-start

commit v2 on v1

v2 whole, which is shorter than its diff:
```python
import functools

import jax
import jax.numpy as jnp
from jax import lax
from jax.experimental import pallas as pl
from jax.experimental.pallas import tpu as pltpu
from jax.sharding import PartitionSpec as P

SOFTENING = 0.0025
MESH = pl.DeviceIdType.MESH
F32, BF16 = jnp.float32, jnp.bfloat16
LANES = 128
GROUP = 16
ACT = 8
STARS = 4096
TILES = STARS // LANES
SLOTS = GROUP * LANES
BLOCK = 256
CHUNK = 2048


def place():
    row = lax.axis_index("row")
    col = lax.axis_index("col")
    core = lax.rem(col, 2)
    return row, col, core, lax.div(col, 2), row * 2 + core


def zy_peer(step):
    row, col, core, zy, rc = place()
    peer = lax.rem(zy + step, GROUP)
    return peer, (row, peer * 2 + core)


def rc_peer(step):
    row, col, core, zy, rc = place()
    peer = lax.rem(rc + step, GROUP)
    return peer, (lax.div(peer, 2), zy * 2 + lax.rem(peer, 2))


def greet():
    barrier = pltpu.get_barrier_semaphore()
    for step in range(1, GROUP):
        for peer in (zy_peer, rc_peer):
            pl.semaphore_signal(barrier, inc=1, device_id=peer(step)[1], device_id_type=MESH)


def await_greetings():
    pl.semaphore_wait(pltpu.get_barrier_semaphore(), 2 * (GROUP - 1))


def wait_bytes(ref, sem):
    pltpu.make_async_copy(ref, ref, sem).wait()


def mm(a, b):
    return jnp.dot(a, b, preferred_element_type=F32)


def mm_t(a, b):
    return lax.dot_general(a, b, (((1,), (1,)), ((), ())), preferred_element_type=F32)


def pieces(value):
    first = value.astype(BF16).astype(F32)
    rest = value - first
    second = rest.astype(BF16).astype(F32)
    return first, second, rest - second


def coordinates(group):
    coarse = jnp.floor(group * 16.0 + 0.5) * 0.0625
    return coarse, pieces(group - coarse)


def scalars(group, coarse, shift):
    sub = lax.broadcasted_iota(jnp.int32, group.shape, 0)
    upper = sub < 3

    def pair(exact, whole):
        exact = jnp.sum(jnp.where(upper, exact, 0.0), axis=0, keepdims=True)
        whole = jnp.sum(jnp.where(upper, whole, 0.0), axis=0, keepdims=True)
        high = exact.astype(BF16).astype(F32)
        return (high, exact - high) + pieces(whole)

    fine = group - coarse
    vel, vel_coarse = pltpu.roll(group, 4, 0), pltpu.roll(coarse, 4, 0)
    square = pair(coarse * coarse, fine * (group + coarse) + jnp.where(sub == 0, shift, 0.0))
    cross = pair(coarse * vel_coarse, fine * vel + coarse * (vel - vel_coarse))
    return square, cross


def stack(rows, shape):
    sub = lax.broadcasted_iota(jnp.int32, shape, 0)
    total = jnp.zeros(shape, F32)
    for at, row in enumerate(rows):
        total = jnp.where(sub == at, row, total)
    return total


def source_features(group):
    coarse, (one, two, three) = coordinates(group)
    square, cross = scalars(group, coarse, 0.0)
    exact = stack(square[0:2] + (1.0, 1.0) + cross[0:2] + (1.0, 1.0), group.shape)
    rest = stack(square[2:5] + (1.0,) + cross[2:5] + (1.0,), group.shape)
    more = stack((1.0, 1.0, 0.0, 0.0, 1.0, 1.0, 0.0, 0.0), group.shape)
    none = jnp.zeros_like(group)
    return [exact, coarse, rest, more, coarse, coarse, coarse, one, two, three, one, one, two, two, none, none]


def target_features(group):
    coarse, (one, two, three) = coordinates(group)
    square, cross = scalars(group, coarse, SOFTENING)
    sub = lax.broadcasted_iota(jnp.int32, group.shape, 0)
    none = jnp.zeros_like(group)

    def tail(scalar, at):
        pad, rest = (0.0,) * at, (0.0,) * (4 - at)
        exact = stack(pad + (1.0, 1.0) + scalar[0:2] + rest, group.shape)
        fine = stack(pad + (1.0, 1.0, 1.0) + scalar[2:3] + rest, group.shape)
        more = stack(pad + scalar[3:5] + (0.0, 0.0) + rest, group.shape)
        return exact, fine, more

    def weights(change, scalar, at):
        exact, fine, more = tail(scalar, at)
        c, o, t, h = change(coarse), change(one), change(two), change(three)
        rows = [exact, c, fine, more, o, t, h, c, c, c, o, t, o, t, none, none]
        return jnp.concatenate(rows, 0).astype(BF16)

    near = weights(lambda v: jnp.where(sub < 3, -2.0 * v, 0.0), square, 0)
    along = weights(lambda v: -pltpu.roll(v, 4, 0), cross, 4)
    return near, along


def prepare_tile(tile, stars, mass_ref, feature_ref, moment_ref):
    cols = pl.ds(pl.multiple_of(tile * LANES, LANES), LANES)
    group = stars[:, cols]
    rows = jnp.concatenate(source_features(group), 0)
    feature_ref[cols, :] = rows.T.astype(BF16)
    sub = lax.broadcasted_iota(jnp.int32, group.shape, 0)
    moment = mass_ref[pl.ds(tile, 1), :] * jnp.where(sub == 3, 1.0, group)
    one, two, three = pieces(moment)
    moment_ref[:, cols] = jnp.concatenate([one, two, three, jnp.zeros_like(one)], 0).astype(BF16)


def gather_kernel(index_ref, count_ref, pos_ref, vel_ref, acc_ref, jerk_ref, mass_ref, elapsed_ref,
                  feature_ref, moment_ref, all_ref, rank_ref, live_ref,
                  stars, mine, near, send_sem, recv_sem):
    row, col, core, zy, rc = place()
    greet()
    stars[...] = jnp.zeros_like(stars)
    for tile in range(TILES):
        cols = pl.ds(tile * LANES, LANES)
        dt = elapsed_ref[tile:tile + 1, :]
        vel, acc, jerk = vel_ref[:, cols], acc_ref[:, cols], jerk_ref[:, cols]
        stars[0:3, cols] = pos_ref[:, cols] + dt * (vel + dt * (0.5 * acc + dt * (jerk * (1.0 / 6.0))))
        stars[4:7, cols] = vel + dt * (acc + dt * (0.5 * jerk))
    lane = lax.broadcasted_iota(jnp.int32, (8, LANES), 1)
    sub = lax.broadcasted_iota(jnp.int32, (8, LANES), 0)
    total = jnp.zeros((8, LANES), F32)
    for slot in range(ACT):
        away = lane - index_ref[slot]
        picked = jnp.zeros((8, LANES), F32)
        for tile in range(TILES):
            picked = jnp.where(away == -tile * LANES, stars[:, pl.ds(tile * LANES, LANES)], picked)
        value = jnp.sum(picked, axis=1, keepdims=True)
        value = jnp.where(sub == 3, jnp.where(slot < count_ref[0], 1.0, 0.0), value)
        total = jnp.where(lane == zy * ACT + slot, value, total)
    mine[...] = total
    await_greetings()
    for step in range(1, GROUP):
        peer, device = zy_peer(step)
        pltpu.make_async_remote_copy(
            src_ref=mine, dst_ref=near.at[step - 1],
            send_sem=send_sem.at[0], recv_sem=recv_sem.at[0],
            device_id=device, device_id_type=MESH).start()

    def prepare(tile, carry):
        prepare_tile(tile, stars, mass_ref, feature_ref, moment_ref)
        return carry

    lax.fori_loop(0, TILES // 2, prepare, 0, unroll=2)
    wait_bytes(near, recv_sem.at[0])
    for step in range(1, GROUP):
        total = total + near[step - 1]
    all_ref[pl.ds(rc, 1)] = total[None]
    for step in range(1, GROUP):
        peer, device = rc_peer(step)
        pltpu.make_async_remote_copy(
            src_ref=all_ref.at[rc], dst_ref=all_ref.at[rc],
            send_sem=send_sem.at[1], recv_sem=recv_sem.at[1],
            device_id=device, device_id_type=MESH).start()
    lax.fori_loop(TILES // 2, TILES, prepare, 0, unroll=2)
    wait_bytes(near, send_sem.at[0])
    wait_bytes(near, recv_sem.at[1])
    alive = jnp.concatenate([all_ref[g, 3:4, :] for g in range(GROUP)], 0)
    before = lax.broadcasted_iota(jnp.int32, (LANES, LANES), 0)
    after = lax.broadcasted_iota(jnp.int32, (LANES, LANES), 1)
    inside = mm(alive.astype(BF16), jnp.where(before < after, 1.0, 0.0).astype(BF16))
    sums = mm(alive.astype(BF16), jnp.ones((LANES, LANES), BF16))
    earlier = jnp.where((after < before) & (after < GROUP), 1.0, 0.0)[0:GROUP, 0:GROUP]
    ahead = mm(earlier.astype(BF16), sums.astype(BF16))
    rank_ref[...] = jnp.where(alive > 0.0, inside + ahead, -1.0)
    live_ref[...] = (ahead + sums)[GROUP - 1:GROUP, :].astype(jnp.int32)
    wait_bytes(near, send_sem.at[1])


def force_kernel(live_ref, feature_ref, moment_ref, all_ref, rank_ref, out_ref, hot):
    out_ref[...] = jnp.zeros_like(out_ref)
    spread = jnp.concatenate([all_ref[g] for g in range(GROUP)], 1)
    slots = jnp.concatenate(list(pieces(spread)) + [jnp.zeros_like(spread)], 0).astype(BF16)
    target = lax.broadcasted_iota(jnp.int32, (BLOCK, LANES), 0).astype(F32)
    sub = lax.broadcasted_iota(jnp.int32, (8, BLOCK), 0)

    def block(index, carry):
        wanted = target + (index * BLOCK).astype(F32)
        for g in range(GROUP):
            hot[:, g * LANES:(g + 1) * LANES] = jnp.where(
                wanted == rank_ref[g:g + 1, :], 1.0, 0.0).astype(BF16)
        packed = mm_t(slots, hot[...])
        packed = packed[0:8] + packed[8:16] + packed[16:24]
        packed = jnp.where((sub == 3) | (sub == 7), 0.0, packed)
        near, along = target_features(packed)

        def chunk(step, sums):
            rows = pl.ds(pl.multiple_of(step * CHUNK, CHUNK), CHUNK)
            r2 = mm(feature_ref[rows, :], near)
            dot = mm(feature_ref[rows, :], along)
            inv = lax.rsqrt(r2)
            inv2 = inv * inv
            w = inv * inv2
            u = (w * inv2) * dot
            moments = moment_ref[:, rows]
            new = []
            for value, old in zip((w, u), sums):
                high = value.astype(BF16)
                low = (value - high.astype(F32)).astype(BF16)
                new.append(old + (mm(moments, high) + mm(moments, low)))
            return tuple(new)

        zero = jnp.zeros((32, BLOCK), F32)
        sums = lax.fori_loop(0, STARS // CHUNK, chunk, (zero, zero))
        first, second = [s[0:8] + s[8:16] + s[16:24] for s in sums]
        first = first - packed * first[3:4, :]
        second = second - packed * second[3:4, :]
        force = first - 3.0 * jnp.where(sub >= 4, pltpu.roll(second, 4, 0), 0.0)
        force = jnp.concatenate(list(pieces(force)) + [jnp.zeros_like(force)], 0).astype(BF16)
        back = mm(force, hot[...])
        back = back[0:8] + back[8:16] + back[16:24]
        for g in range(GROUP):
            out_ref[g] += back[:, g * LANES:(g + 1) * LANES]
        return carry

    lax.fori_loop(0, lax.div(live_ref[0, 0] + (BLOCK - 1), BLOCK), block, 0)


def scatter_kernel(count_ref, part_ref, accel_ref, jerk_ref, first, second, summed, send_sem, recv_sem):
    row, col, core, zy, rc = place()
    greet()
    await_greetings()
    for step in range(1, GROUP):
        peer, device = rc_peer(step)
        pltpu.make_async_remote_copy(
            src_ref=part_ref.at[peer], dst_ref=first.at[step - 1],
            send_sem=send_sem.at[0], recv_sem=recv_sem.at[0],
            device_id=device, device_id_type=MESH).start()
    total = part_ref[rc]
    wait_bytes(first, recv_sem.at[0])
    for step in range(1, GROUP):
        total = total + first[step - 1]
    summed[...] = total
    for step in range(1, GROUP):
        peer, device = zy_peer(step)
        pltpu.make_async_remote_copy(
            src_ref=summed, dst_ref=second.at[step - 1],
            send_sem=send_sem.at[1], recv_sem=recv_sem.at[1],
            device_id=device, device_id_type=MESH).start()
    wait_bytes(second, recv_sem.at[1])
    for step in range(1, GROUP):
        total = total + second[step - 1]
    mine = pltpu.roll(total, lax.rem(LANES - zy * ACT, LANES), 1)
    lane = lax.broadcasted_iota(jnp.int32, (8, LANES), 1)
    mine = jnp.where(lane < count_ref[0], mine, 0.0)
    accel_ref[...] = mine[0:3, 0:ACT]
    jerk_ref[...] = mine[4:7, 0:ACT]
    wait_bytes(first, send_sem.at[0])
    wait_bytes(second, send_sem.at[1])


def local(position, velocity, accel_old, jerk_old, mass, elapsed, active_index, active_count):
    vmem = pl.BlockSpec(memory_space=pltpu.VMEM)
    smem = pl.BlockSpec(memory_space=pltpu.SMEM)
    tiles = (GROUP, 8, LANES)
    features, moments, everyone, rank, live = pl.pallas_call(
        gather_kernel,
        out_shape=(
            jax.ShapeDtypeStruct((STARS, LANES), BF16),
            jax.ShapeDtypeStruct((32, STARS), BF16),
            jax.ShapeDtypeStruct(tiles, F32),
            jax.ShapeDtypeStruct((GROUP, LANES), F32),
            jax.ShapeDtypeStruct((1, LANES), jnp.int32),
        ),
        in_specs=[smem, smem] + [vmem] * 6,
        out_specs=(vmem,) * 5,
        scratch_shapes=[
            pltpu.VMEM((8, STARS), F32),
            pltpu.VMEM((8, LANES), F32),
            pltpu.VMEM((GROUP - 1, 8, LANES), F32),
            pltpu.SemaphoreType.DMA((2,)),
            pltpu.SemaphoreType.DMA((2,)),
        ],
        compiler_params=pltpu.CompilerParams(collective_id=0, has_side_effects=True),
        name="gather_targets",
    )(active_index, active_count, position, velocity, accel_old, jerk_old,
      mass.reshape(TILES, LANES), elapsed.reshape(TILES, LANES))
    parts = pl.pallas_call(
        force_kernel,
        out_shape=jax.ShapeDtypeStruct(tiles, F32),
        in_specs=[smem] + [vmem] * 4,
        out_specs=vmem,
        scratch_shapes=[pltpu.VMEM((BLOCK, SLOTS), BF16)],
        compiler_params=pltpu.CompilerParams(vmem_limit_bytes=40 * 2**20),
        name="forces",
    )(live, features, moments, everyone, rank)
    return pl.pallas_call(
        scatter_kernel,
        out_shape=(jax.ShapeDtypeStruct((3, ACT), F32), jax.ShapeDtypeStruct((3, ACT), F32)),
        in_specs=[smem, vmem],
        out_specs=(vmem, vmem),
        scratch_shapes=[
            pltpu.VMEM((GROUP - 1, 8, LANES), F32),
            pltpu.VMEM((GROUP - 1, 8, LANES), F32),
            pltpu.VMEM((8, LANES), F32),
            pltpu.SemaphoreType.DMA((2,)),
            pltpu.SemaphoreType.DMA((2,)),
        ],
        compiler_params=pltpu.CompilerParams(collective_id=1, has_side_effects=True),
        name="scatter_forces",
    )(active_count, parts)


def solution(mesh):
    split = P(None, ("row", "col"))
    flat = P(("row", "col"))
    return jax.shard_map(
        local,
        mesh=mesh,
        in_specs=(split, split, split, split, flat, flat, flat, flat),
        out_specs=(split, split),
        check_vma=False,
    )
```

time: 77.5 us -> 58.2 us (0.75)
  Pallas kernels: 74.1 us -> 50.2 us
  local copies, waits for them, and re-layouts: 1.89 us -> 6.2 us
    pallas_call x2, Pallas kernels: 59.2 us -> 35 us  [the longest x1 23.1 us: local(): pl.pallas_call(gather_kernel, out_shape=(jax.ShapeDtypeStruct((STARS, LAN...]
    unnamed x6 -> x18, local copies, waits for them, and re-layouts: 1.89 us -> 6.2 us
where the time goes in v2:
time: 58.2 us; the launch traced here: 57.8 us
  Pallas kernels  50.2 us (86%)
  local copies, waits for them, and re-layouts  6.2 us (11%)
  between operations  1.34 us (2%)
    pallas_call x1, Pallas kernels, local(): pl.pallas_call(gather_kernel, out_shape=(jax.ShapeDtypeStruct((STARS, LAN...  23.1 us
    pallas_call x1, Pallas kernels, local(): pl.pallas_call(scatter_kernel, out_shape=(jax.ShapeDtypeStruct((3, ACT),...  15.2 us
    pallas_call x1, Pallas kernels, local(): pl.pallas_call(force_kernel, out_shape=jax.ShapeDtypeStruct(tiles, F32),...  11.9 us
    unnamed x18, local copies, waits for them, and re-layouts  6.2 us

profile of v2, /device:TPU:1, one launch (start us, length us, event | category | flops | bytes accessed | tf_op | source)
XLA Modules:
  0.0 57.8 jit_solution(3112089561032730365)
XLA Ops:
  1.3 23.1 %gather_targets.1 = (bf16[4096,128]{1,0:T(8,128)(2,1)}, bf16[32,4096]{1,0:T(8,128)(2,1)}, f32[16,8,128]{2,1,0:T(8,128)}, f32[16,128]{1,0:T(8,128)}, s32[1,128]{1,0:T(1,128)}) custom-call(s32[8]{0:T(128)} %index_ref.1, s32[1]{0:T(128)S(6)} %copy.12.count_ref, f32[3,4096]{1,0:T(4,128)} %pos_ref.1, f32[3,4096]{1,0:T(4,128)} %vel_ref.1, f32[3,4096]{1,0:T(4,128)} %acc_ref.1, ...), custom_call_target="tpu_custom_call" | custom-call | tf_op jit(solution)/shard_map/gather_targets/pallas_call | solution.py:295
  24.4 0.0 copy-start.4
  24.4 0.0 copy-start.5
  24.4 0.7 %copy-done.4 = f32[16,128]{1,0:T(8,128)S(1)} copy-done((f32[16,128]{1,0:T(8,128)S(1)}, f32[16,128]{1,0:T(8,128)}, u32[]{:S(2)}) %copy-start.4) | copy-done | bytes 8216
  25.1 0.0 copy-done.5
  25.1 0.0 copy-start
  25.1 1.2 %copy-done = bf16[4096,128]{1,0:T(8,128)(2,1)S(1)} copy-done((bf16[4096,128]{1,0:T(8,128)(2,1)S(1)}, bf16[4096,128]{1,0:T(8,128)(2,1)}, u32[]{:S(2)}) %copy-start) | copy-done | bytes 1048600
  26.4 0.0 copy-start.1
  26.4 0.9 %copy-done.1 = bf16[32,4096]{1,0:T(8,128)(2,1)S(1)} copy-done((bf16[32,4096]{1,0:T(8,128)(2,1)S(1)}, bf16[32,4096]{1,0:T(8,128)(2,1)}, u32[]{:S(2)}) %copy-start.1) | copy-done | bytes 262168
  27.3 0.0 copy-start.3
  27.3 0.8 %copy-done.3 = f32[16,8,128]{2,1,0:T(8,128)S(1)} copy-done((f32[16,8,128]{2,1,0:T(8,128)S(1)}, f32[16,8,128]{2,1,0:T(8,128)}, u32[]{:S(2)}) %copy-start.3) | copy-done | bytes 65560
  28.1 11.9 %forces.1.part_ref = f32[16,8,128]{2,1,0:T(8,128)S(1)} custom-call(s32[1,128]{1,0:T(1,128)S(1)} %copy-done.5, bf16[4096,128]{1,0:T(8,128)(2,1)S(1)} %copy-done, bf16[32,4096]{1,0:T(8,128)(2,1)S(1)} %copy-done.1, f32[16,8,128]{2,1,0:T(8,128)S(1)} %copy-done.3, f32[16,128]{1,0:T(8,128)S(1)} %copy-done.4), custom_call_target="tpu_custom_call" | custom-call | tf_op jit(solution)/shard_map/forces/pallas_call | solution.py:317
  40.0 0.0 copy-start.2
  40.0 0.6 %copy-done.2 = f32[16,8,128]{2,1,0:T(8,128)} copy-done((f32[16,8,128]{2,1,0:T(8,128)}, f32[16,8,128]{2,1,0:T(8,128)S(1)}, u32[]{:S(2)}) %copy-start.2) | copy-done | bytes 65560
  40.7 15.2 %scatter_forces.1 = (f32[3,8]{1,0:T(4,128)}, f32[3,8]{1,0:T(4,128)}) custom-call(s32[1]{0:T(128)S(6)} %copy.12.count_ref, f32[16,8,128]{2,1,0:T(8,128)} %copy-done.2), custom_call_target="tpu_custom_call" | custom-call | tf_op jit(solution)/shard_map/scatter_forces/pallas_call | solution.py:326
  55.9 0.0 copy-start.7
  55.9 0.6 %copy-done.7 = f32[3,8]{1,0:T(4,128)S(1)} copy-done((f32[3,8]{1,0:T(4,128)S(1)}, f32[3,8]{1,0:T(4,128)}, u32[]{:S(2)}) %copy-start.7) | copy-done | bytes 120
  56.5 0.0 copy-start.6
  56.5 0.6 copy.13
  57.1 0.1 copy-done.6
  57.2 0.6 copy.14
Async XLA Ops:
  24.4 0.7 %copy-start.4 = (f32[16,128]{1,0:T(8,128)S(1)}, f32[16,128]{1,0:T(8,128)}, u32[]{:S(2)}) copy-start(f32[16,128]{1,0:T(8,128)} %get-tuple-element.11.rank_ref) | copy-start | bytes 24580
  24.4 0.7 %copy-start.5 = (s32[1,128]{1,0:T(1,128)S(1)}, s32[1,128]{1,0:T(1,128)}, u32[]{:S(2)}) copy-start(s32[1,128]{1,0:T(1,128)} %get-tuple-element.7.live_ref) | copy-start | bytes 1540
  25.1 1.2 %copy-start = (bf16[4096,128]{1,0:T(8,128)(2,1)S(1)}, bf16[4096,128]{1,0:T(8,128)(2,1)}, u32[]{:S(2)}) copy-start(bf16[4096,128]{1,0:T(8,128)(2,1)} %get-tuple-element.8.feature_ref) | copy-start | bytes 3145732
  26.4 0.9 %copy-start.1 = (bf16[32,4096]{1,0:T(8,128)(2,1)S(1)}, bf16[32,4096]{1,0:T(8,128)(2,1)}, u32[]{:S(2)}) copy-start(bf16[32,4096]{1,0:T(8,128)(2,1)} %get-tuple-element.9.moment_ref) | copy-start | bytes 786436
  27.3 0.8 %copy-start.3 = (f32[16,8,128]{2,1,0:T(8,128)S(1)}, f32[16,8,128]{2,1,0:T(8,128)}, u32[]{:S(2)}) copy-start(f32[16,8,128]{2,1,0:T(8,128)} %get-tuple-element.10.all_ref) | copy-start | bytes 196612
  40.0 0.6 %copy-start.2 = (f32[16,8,128]{2,1,0:T(8,128)}, f32[16,8,128]{2,1,0:T(8,128)S(1)}, u32[]{:S(2)}) copy-start(f32[16,8,128]{2,1,0:T(8,128)S(1)} %forces.1.part_ref) | copy-start | bytes 196612
  55.9 0.7 %copy-start.7 = (f32[3,8]{1,0:T(4,128)S(1)}, f32[3,8]{1,0:T(4,128)}, u32[]{:S(2)}) copy-start(f32[3,8]{1,0:T(4,128)} %get-tuple-element.14) | copy-start | bytes 292
  56.5 0.7 %copy-start.6 = (f32[3,8]{1,0:T(4,128)S(1)}, f32[3,8]{1,0:T(4,128)}, u32[]{:S(2)}) copy-start(f32[3,8]{1,0:T(4,128)} %get-tuple-element.15) | copy-start | bytes 292

commit v3 on v2

--- a/solution.py
+++ b/solution.py
@@ -17,7 +17,8 @@
 TILES = STARS // LANES
 SLOTS = GROUP * LANES
 BLOCK = 256
-CHUNK = 2048
+CHUNK = 4096
+SIZES = (3, 4, 8)
 
 
 def place():
@@ -144,11 +145,22 @@
     moment_ref[:, cols] = jnp.concatenate([one, two, three, jnp.zeros_like(one)], 0).astype(BF16)
 
 
-def gather_kernel(index_ref, count_ref, pos_ref, vel_ref, acc_ref, jerk_ref, mass_ref, elapsed_ref,
-                  feature_ref, moment_ref, all_ref, rank_ref, live_ref,
-                  stars, mine, near, send_sem, recv_sem):
+def gather_kernel(index_ref, count_ref, pos_hbm, vel_hbm, acc_hbm, jerk_hbm, mass_hbm, elapsed_hbm,
+                  feature_ref, moment_ref, all_ref, rank_ref, choice_ref,
+                  pos_ref, vel_ref, acc_ref, jerk_ref, mass_ref, elapsed_ref,
+                  stars, mine, near, load_sem, send_sem, recv_sem):
+    loads = [
+        pltpu.make_async_copy(src, dst, load_sem.at[at])
+        for at, (src, dst) in enumerate((
+            (pos_hbm, pos_ref), (vel_hbm, vel_ref), (acc_hbm, acc_ref), (jerk_hbm, jerk_ref),
+            (mass_hbm, mass_ref), (elapsed_hbm, elapsed_ref)))
+    ]
+    for load in loads:
+        load.start()
     row, col, core, zy, rc = place()
     greet()
+    for load in loads:
+        load.wait()
     stars[...] = jnp.zeros_like(stars)
     for tile in range(TILES):
         cols = pl.ds(tile * LANES, LANES)
@@ -202,19 +214,22 @@
     earlier = jnp.where((after < before) & (after < GROUP), 1.0, 0.0)[0:GROUP, 0:GROUP]
     ahead = mm(earlier.astype(BF16), sums.astype(BF16))
     rank_ref[...] = jnp.where(alive > 0.0, inside + ahead, -1.0)
-    live_ref[...] = (ahead + sums)[GROUP - 1:GROUP, :].astype(jnp.int32)
+    live = (ahead + sums)[GROUP - 1, 0].astype(jnp.int32)
+    choice_ref[0] = sum((live > BLOCK * size).astype(jnp.int32) for size in SIZES[:-1])
     wait_bytes(near, send_sem.at[1])
 
 
-def force_kernel(live_ref, feature_ref, moment_ref, all_ref, rank_ref, out_ref, hot):
-    out_ref[...] = jnp.zeros_like(out_ref)
+def force_kernel(blocks, count_ref, feature_ref, moment_ref, all_ref, rank_ref, out_ref,
+                 part_ref, hot, first, second, summed, send_sem, recv_sem):
+    greet()
+    part_ref[...] = jnp.zeros_like(part_ref)
     spread = jnp.concatenate([all_ref[g] for g in range(GROUP)], 1)
     slots = jnp.concatenate(list(pieces(spread)) + [jnp.zeros_like(spread)], 0).astype(BF16)
     target = lax.broadcasted_iota(jnp.int32, (BLOCK, LANES), 0).astype(F32)
     sub = lax.broadcasted_iota(jnp.int32, (8, BLOCK), 0)
 
     def block(index, carry):
-        wanted = target + (index * BLOCK).astype(F32)
+        wanted = target + lax.convert_element_type(index * BLOCK, F32)
         for g in range(GROUP):
             hot[:, g * LANES:(g + 1) * LANES] = jnp.where(
                 wanted == rank_ref[g:g + 1, :], 1.0, 0.0).astype(BF16)
@@ -240,24 +255,20 @@
             return tuple(new)
 
         zero = jnp.zeros((32, BLOCK), F32)
-        sums = lax.fori_loop(0, STARS // CHUNK, chunk, (zero, zero))
-        first, second = [s[0:8] + s[8:16] + s[16:24] for s in sums]
-        first = first - packed * first[3:4, :]
-        second = second - packed * second[3:4, :]
-        force = first - 3.0 * jnp.where(sub >= 4, pltpu.roll(second, 4, 0), 0.0)
+        sums = chunk(0, (zero, zero))
+        by_w, by_u = [s[0:8] + s[8:16] + s[16:24] for s in sums]
+        by_w = by_w - packed * by_w[3:4, :]
+        by_u = by_u - packed * by_u[3:4, :]
+        force = by_w - 3.0 * jnp.where(sub >= 4, pltpu.roll(by_u, 4, 0), 0.0)
         force = jnp.concatenate(list(pieces(force)) + [jnp.zeros_like(force)], 0).astype(BF16)
         back = mm(force, hot[...])
         back = back[0:8] + back[8:16] + back[16:24]
         for g in range(GROUP):
-            out_ref[g] += back[:, g * LANES:(g + 1) * LANES]
+            part_ref[g] += back[:, g * LANES:(g + 1) * LANES]
         return carry
 
-    lax.fori_loop(0, lax.div(live_ref[0, 0] + (BLOCK - 1), BLOCK), block, 0)
-
-
-def scatter_kernel(count_ref, part_ref, accel_ref, jerk_ref, first, second, summed, send_sem, recv_sem):
+    lax.fori_loop(0, blocks, block, 0)
     row, col, core, zy, rc = place()
-    greet()
     await_greetings()
     for step in range(1, GROUP):
         peer, device = rc_peer(step)
@@ -281,63 +292,75 @@
         total = total + second[step - 1]
     mine = pltpu.roll(total, lax.rem(LANES - zy * ACT, LANES), 1)
     lane = lax.broadcasted_iota(jnp.int32, (8, LANES), 1)
-    mine = jnp.where(lane < count_ref[0], mine, 0.0)
-    accel_ref[...] = mine[0:3, 0:ACT]
-    jerk_ref[...] = mine[4:7, 0:ACT]
+    out_ref[...] = jnp.where(lane < count_ref[0], mine, 0.0)
     wait_bytes(first, send_sem.at[0])
     wait_bytes(second, send_sem.at[1])
+
+
+def finish_kernel(force_ref, accel_ref, jerk_ref):
+    accel_ref[...] = force_ref[0:3, 0:ACT]
+    jerk_ref[...] = force_ref[4:7, 0:ACT]
 
 
 def local(position, velocity, accel_old, jerk_old, mass, elapsed, active_index, active_count):
     vmem = pl.BlockSpec(memory_space=pltpu.VMEM)
     smem = pl.BlockSpec(memory_space=pltpu.SMEM)
+    hbm = pl.BlockSpec(memory_space=pltpu.HBM)
     tiles = (GROUP, 8, LANES)
-    features, moments, everyone, rank, live = pl.pallas_call(
+    features, moments, everyone, rank, choice = pl.pallas_call(
         gather_kernel,
         out_shape=(
             jax.ShapeDtypeStruct((STARS, LANES), BF16),
             jax.ShapeDtypeStruct((32, STARS), BF16),
             jax.ShapeDtypeStruct(tiles, F32),
             jax.ShapeDtypeStruct((GROUP, LANES), F32),
-            jax.ShapeDtypeStruct((1, LANES), jnp.int32),
+            jax.ShapeDtypeStruct((1,), jnp.int32),
         ),
-        in_specs=[smem, smem] + [vmem] * 6,
-        out_specs=(vmem,) * 5,
-        scratch_shapes=[
+        in_specs=[smem, smem] + [hbm] * 6,
+        out_specs=(vmem,) * 4 + (smem,),
+        scratch_shapes=[pltpu.VMEM((3, STARS), F32)] * 4 + [pltpu.VMEM((TILES, LANES), F32)] * 2 + [
             pltpu.VMEM((8, STARS), F32),
             pltpu.VMEM((8, LANES), F32),
             pltpu.VMEM((GROUP - 1, 8, LANES), F32),
+            pltpu.SemaphoreType.DMA((6,)),
             pltpu.SemaphoreType.DMA((2,)),
             pltpu.SemaphoreType.DMA((2,)),
         ],
-        compiler_params=pltpu.CompilerParams(collective_id=0, has_side_effects=True),
+        compiler_params=pltpu.CompilerParams(
+            collective_id=0, has_side_effects=True, vmem_limit_bytes=8 * 2**20),
         name="gather_targets",
     )(active_index, active_count, position, velocity, accel_old, jerk_old,
       mass.reshape(TILES, LANES), elapsed.reshape(TILES, LANES))
-    parts = pl.pallas_call(
-        force_kernel,
-        out_shape=jax.ShapeDtypeStruct(tiles, F32),
-        in_specs=[smem] + [vmem] * 4,
-        out_specs=vmem,
-        scratch_shapes=[pltpu.VMEM((BLOCK, SLOTS), BF16)],
-        compiler_params=pltpu.CompilerParams(vmem_limit_bytes=40 * 2**20),
-        name="forces",
-    )(live, features, moments, everyone, rank)
+
+    def forces(at):
+        return pl.pallas_call(
+            functools.partial(force_kernel, SIZES[at]),
+            out_shape=jax.ShapeDtypeStruct((8, LANES), F32),
+            in_specs=[smem] + [vmem] * 4,
+            out_specs=vmem,
+            scratch_shapes=[
+                pltpu.VMEM(tiles, F32),
+                pltpu.VMEM((BLOCK, SLOTS), BF16),
+                pltpu.VMEM((GROUP - 1, 8, LANES), F32),
+                pltpu.VMEM((GROUP - 1, 8, LANES), F32),
+                pltpu.VMEM((8, LANES), F32),
+                pltpu.SemaphoreType.DMA((2,)),
+                pltpu.SemaphoreType.DMA((2,)),
+            ],
+            compiler_params=pltpu.CompilerParams(
+                collective_id=1 + at, has_side_effects=True, vmem_limit_bytes=24 * 2**20),
+            name="forces_%d" % SIZES[at],
+        )
+
+    branches = [forces(at) for at in range(len(SIZES))]
+    mine = lax.switch(choice[0], branches, active_count, features, moments, everyone, rank)
     return pl.pallas_call(
-        scatter_kernel,
+        finish_kernel,
         out_shape=(jax.ShapeDtypeStruct((3, ACT), F32), jax.ShapeDtypeStruct((3, ACT), F32)),
-        in_specs=[smem, vmem],
+        in_specs=[vmem],
         out_specs=(vmem, vmem),
-        scratch_shapes=[
-            pltpu.VMEM((GROUP - 1, 8, LANES), F32),
-            pltpu.VMEM((GROUP - 1, 8, LANES), F32),
-            pltpu.VMEM((8, LANES), F32),
-            pltpu.SemaphoreType.DMA((2,)),
-            pltpu.SemaphoreType.DMA((2,)),
-        ],
-        compiler_params=pltpu.CompilerParams(collective_id=1, has_side_effects=True),
-        name="scatter_forces",
-    )(active_count, parts)
+        name="finish",
+    )(mine)
 
 
 def solution(mesh):

time: 58.2 us -> 53.1 us (0.912)
  Pallas kernels: 50.2 us -> 45 us
  local copies, waits for them, and re-layouts: 6.2 us -> 5.44 us
  between operations: 1.34 us -> 1.94 us
    pallas_call x2, Pallas kernels: 27.1 us -> 22.5 us  [the longest x1 21.9 us: local(): lax.switch(choice[0], branches, active_count, features, moments, everyone...]
    unnamed x18 -> x14, local copies, waits for them, and re-layouts: 6.2 us -> 5.44 us
    pallas_call x1, Pallas kernels: 23.1 us -> 22.5 us  [local(): pl.pallas_call(gather_kernel, out_shape=(jax.ShapeDtypeStruct((STARS, LAN...]
where the time goes in v3:
time: 53.1 us; the launch traced here: 52.6 us
  Pallas kernels  45 us (85%)
  local copies, waits for them, and re-layouts  5.44 us (10%)
  between operations  1.94 us (4%)
    pallas_call x1, Pallas kernels, local(): pl.pallas_call(gather_kernel, out_shape=(jax.ShapeDtypeStruct((STARS, LAN...  22.5 us
    pallas_call x1, Pallas kernels, local(): lax.switch(choice[0], branches, active_count, features, moments, everyone...  21.9 us
    unnamed x14, local copies, waits for them, and re-layouts  5.44 us

profile of v3, /device:TPU:1, one launch (start us, length us, event | category | flops | bytes accessed | tf_op | source)
XLA Modules:
  0.0 52.6 jit_solution(6201879217437229100)
XLA Ops:
  1.3 0.0 copy-start.6
  1.3 0.6 %copy-done.6 = s32[8]{0:T(128)S(1)} copy-done((s32[8]{0:T(128)S(1)}, s32[8]{0:T(128)}, u32[]{:S(2)}) %copy-start.6) | copy-done | bytes 56
  1.9 0.0 copy-start
  1.9 0.8 %copy-done = f32[3,4096]{1,0:T(4,128)S(1)} copy-done((f32[3,4096]{1,0:T(4,128)S(1)}, f32[3,4096]{1,0:T(4,128)}, u32[]{:S(2)}) %copy-start) | copy-done | bytes 49176
  2.8 0.0 copy-start.1
  2.8 0.8 %copy-done.1 = f32[3,4096]{1,0:T(4,128)S(1)} copy-done((f32[3,4096]{1,0:T(4,128)S(1)}, f32[3,4096]{1,0:T(4,128)}, u32[]{:S(2)}) %copy-start.1) | copy-done | bytes 49176
  3.6 0.0 copy-start.2
  3.6 0.8 %copy-done.2 = f32[3,4096]{1,0:T(4,128)S(1)} copy-done((f32[3,4096]{1,0:T(4,128)S(1)}, f32[3,4096]{1,0:T(4,128)}, u32[]{:S(2)}) %copy-start.2) | copy-done | bytes 49176
  4.5 0.0 copy-start.3
  4.5 0.8 %copy-done.3 = f32[3,4096]{1,0:T(4,128)S(1)} copy-done((f32[3,4096]{1,0:T(4,128)S(1)}, f32[3,4096]{1,0:T(4,128)}, u32[]{:S(2)}) %copy-start.3) | copy-done | bytes 49176
  5.3 0.0 copy-start.4
  5.3 0.7 %copy-done.4 = f32[4096]{0:T(1024)S(1)} copy-done((f32[4096]{0:T(1024)S(1)}, f32[4096]{0:T(1024)}, u32[]{:S(2)}) %copy-start.4) | copy-done | bytes 16408
  6.0 0.0 copy-start.5
  6.0 0.7 %copy-done.5 = f32[4096]{0:T(1024)S(1)} copy-done((f32[4096]{0:T(1024)S(1)}, f32[4096]{0:T(1024)}, u32[]{:S(2)}) %copy-start.5) | copy-done | bytes 16408
  6.7 22.5 %gather_targets.1 = (bf16[4096,128]{1,0:T(8,128)(2,1)S(1)}, bf16[32,4096]{1,0:T(8,128)(2,1)S(1)}, f32[16,8,128]{2,1,0:T(8,128)S(1)}, f32[16,128]{1,0:T(8,128)S(1)}, s32[1]{0:T(128)}) custom-call(s32[8]{0:T(128)S(1)} %copy-done.6, s32[1]{0:T(128)S(6)} %copy.13.count_ref, f32[3,4096]{1,0:T(4,128)S(1)} %copy-done, f32[3,4096]{1,0:T(4,128)S(1)} %copy-done.1, ...), custom_call_target="tpu_custom_call" | custom-call | tf_op jit(solution)/shard_map/gather_targets/pallas_call | solution.py:310
  29.8 22.1 %conditional.1 = (f32[8,128]{1,0:T(8,128)S(1)}) conditional(s32[]{:T(128)} %bitcast.2, (s32[1]{0:T(128)}, bf16[4096,128]{1,0:T(8,128)(2,1)S(1)}, bf16[32,4096]{1,0:T(8,128)(2,1)S(1)}, f32[16,8,128]{2,1,0:T(8,128)S(1)}, f32[16,128]{1,0:T(8,128)S(1)}) %tuple.16, (s32[1]{0:T(128)}, bf16[4096,128]{1,0:T(8,128)(2,1)S(1)}, ...), branch_computations={%region_0.0_spmd, %region_1.0_spmd, %region_2.0_spmd} | conditional | bytes 8 | solution.py:356
  29.9 21.9 %forces_3.1 = f32[8,128]{1,0:T(8,128)S(1)} custom-call(s32[1]{0:T(128)} %get-tuple-element.14.count_ref, bf16[4096,128]{1,0:T(8,128)(2,1)S(1)} %get-tuple-element.24.feature_ref, bf16[32,4096]{1,0:T(8,128)(2,1)S(1)} %get-tuple-element.36.moment_ref, f32[16,8,128]{2,1,0:T(8,128)S(1)} %get-tuple-element.37.all_ref, f32[16,128]{1,0:T(8,128)S(1)} %get-tuple-element.38.rank_ref), custom_call_target="tpu_custom_call" | custom-call | tf_op jit(solution)/shard_map/cond/branch_0_fun/forces_3/pallas_call | solution.py:356
  52.0 0.6 %finish.1 = (f32[3,8]{1,0:T(4,128)}, f32[3,8]{1,0:T(4,128)}) custom-call(f32[8,128]{1,0:T(8,128)S(1)} %get-tuple-element.61.force_ref), custom_call_target="tpu_custom_call" | custom-call | tf_op jit(solution)/shard_map/finish/pallas_call | solution.py:357
Async XLA Ops:
  1.3 0.7 %copy-start.6 = (s32[8]{0:T(128)S(1)}, s32[8]{0:T(128)}, u32[]{:S(2)}) copy-start(s32[8]{0:T(128)} %index_ref.1) | copy-start | bytes 100
  1.9 0.8 %copy-start = (f32[3,4096]{1,0:T(4,128)S(1)}, f32[3,4096]{1,0:T(4,128)}, u32[]{:S(2)}) copy-start(f32[3,4096]{1,0:T(4,128)} %pos_hbm.1) | copy-start | bytes 147460
  2.8 0.8 %copy-start.1 = (f32[3,4096]{1,0:T(4,128)S(1)}, f32[3,4096]{1,0:T(4,128)}, u32[]{:S(2)}) copy-start(f32[3,4096]{1,0:T(4,128)} %vel_hbm.1) | copy-start | bytes 147460
  3.6 0.8 %copy-start.2 = (f32[3,4096]{1,0:T(4,128)S(1)}, f32[3,4096]{1,0:T(4,128)}, u32[]{:S(2)}) copy-start(f32[3,4096]{1,0:T(4,128)} %acc_hbm.1) | copy-start | bytes 147460
  4.5 0.8 %copy-start.3 = (f32[3,4096]{1,0:T(4,128)S(1)}, f32[3,4096]{1,0:T(4,128)}, u32[]{:S(2)}) copy-start(f32[3,4096]{1,0:T(4,128)} %jerk_hbm.1) | copy-start | bytes 147460
  5.3 0.7 %copy-start.4 = (f32[4096]{0:T(1024)S(1)}, f32[4096]{0:T(1024)}, u32[]{:S(2)}) copy-start(f32[4096]{0:T(1024)} %param.15) | copy-start | bytes 49156
  6.0 0.7 %copy-start.5 = (f32[4096]{0:T(1024)S(1)}, f32[4096]{0:T(1024)}, u32[]{:S(2)}) copy-start(f32[4096]{0:T(1024)} %param.16) | copy-start | bytes 49156

commit v4 on v3

--- a/solution.py
+++ b/solution.py
@@ -15,9 +15,7 @@
 ACT = 8
 STARS = 4096
 TILES = STARS // LANES
-SLOTS = GROUP * LANES
 BLOCK = 256
-CHUNK = 4096
 SIZES = (3, 4, 8)
 
 
@@ -213,61 +211,69 @@
     sums = mm(alive.astype(BF16), jnp.ones((LANES, LANES), BF16))
     earlier = jnp.where((after < before) & (after < GROUP), 1.0, 0.0)[0:GROUP, 0:GROUP]
     ahead = mm(earlier.astype(BF16), sums.astype(BF16))
-    rank_ref[...] = jnp.where(alive > 0.0, inside + ahead, -1.0)
+    first = ahead - LANES * jnp.floor(ahead * (1.0 / LANES))
+    lead = inside + first
+    rank_ref[0] = jnp.where(alive > 0.0, lead - LANES * jnp.floor(lead * (1.0 / LANES)), -1.0)
+    spot = lax.broadcasted_iota(jnp.int32, (GROUP, LANES), 1).astype(F32)
+    rank_ref[1] = jnp.floor(ahead * (1.0 / LANES)) + jnp.where(spot < first, 1.0, 0.0)
     live = (ahead + sums)[GROUP - 1, 0].astype(jnp.int32)
     choice_ref[0] = sum((live > BLOCK * size).astype(jnp.int32) for size in SIZES[:-1])
     wait_bytes(near, send_sem.at[1])
 
 
+def three_rows(group):
+    return jnp.concatenate(list(pieces(group)) + [jnp.zeros_like(group)], 0).astype(BF16)
+
+
+def joined(rows):
+    return rows[0:8] + rows[8:16] + rows[16:24]
+
+
 def force_kernel(blocks, count_ref, feature_ref, moment_ref, all_ref, rank_ref, out_ref,
-                 part_ref, hot, first, second, summed, send_sem, recv_sem):
+                 part_ref, hot, near_ref, along_ref, target_ref, force_ref,
+                 first, second, summed, send_sem, recv_sem):
     greet()
-    part_ref[...] = jnp.zeros_like(part_ref)
-    spread = jnp.concatenate([all_ref[g] for g in range(GROUP)], 1)
-    slots = jnp.concatenate(list(pieces(spread)) + [jnp.zeros_like(spread)], 0).astype(BF16)
-    target = lax.broadcasted_iota(jnp.int32, (BLOCK, LANES), 0).astype(F32)
+    tiles = blocks * BLOCK // LANES
+    spot = lax.broadcasted_iota(jnp.int32, (LANES, LANES), 0).astype(F32)
+    packed = [jnp.zeros((8, LANES), F32)] * tiles
+    for g in range(GROUP):
+        hot[g] = jnp.where(spot == rank_ref[0, g:g + 1, :], 1.0, 0.0).astype(BF16)
+        chosen = joined(mm_t(three_rows(all_ref[g]), hot[g]))
+        tile = rank_ref[1, g:g + 1, :]
+        packed = [old + jnp.where(tile == at, chosen, 0.0) for at, old in enumerate(packed)]
+    row_id = lax.broadcasted_iota(jnp.int32, (8, LANES), 0)
+    for at in range(tiles):
+        cols = pl.ds(at * LANES, LANES)
+        target = jnp.where((row_id == 3) | (row_id == 7), 0.0, packed[at])
+        target_ref[:, cols] = target
+        near_ref[:, cols], along_ref[:, cols] = target_features(target)
     sub = lax.broadcasted_iota(jnp.int32, (8, BLOCK), 0)
 
     def block(index, carry):
-        wanted = target + lax.convert_element_type(index * BLOCK, F32)
-        for g in range(GROUP):
-            hot[:, g * LANES:(g + 1) * LANES] = jnp.where(
-                wanted == rank_ref[g:g + 1, :], 1.0, 0.0).astype(BF16)
-        packed = mm_t(slots, hot[...])
-        packed = packed[0:8] + packed[8:16] + packed[16:24]
-        packed = jnp.where((sub == 3) | (sub == 7), 0.0, packed)
-        near, along = target_features(packed)
-
-        def chunk(step, sums):
-            rows = pl.ds(pl.multiple_of(step * CHUNK, CHUNK), CHUNK)
-            r2 = mm(feature_ref[rows, :], near)
-            dot = mm(feature_ref[rows, :], along)
-            inv = lax.rsqrt(r2)
-            inv2 = inv * inv
-            w = inv * inv2
-            u = (w * inv2) * dot
-            moments = moment_ref[:, rows]
-            new = []
-            for value, old in zip((w, u), sums):
-                high = value.astype(BF16)
-                low = (value - high.astype(F32)).astype(BF16)
-                new.append(old + (mm(moments, high) + mm(moments, low)))
-            return tuple(new)
-
-        zero = jnp.zeros((32, BLOCK), F32)
-        sums = chunk(0, (zero, zero))
-        by_w, by_u = [s[0:8] + s[8:16] + s[16:24] for s in sums]
-        by_w = by_w - packed * by_w[3:4, :]
-        by_u = by_u - packed * by_u[3:4, :]
-        force = by_w - 3.0 * jnp.where(sub >= 4, pltpu.roll(by_u, 4, 0), 0.0)
-        force = jnp.concatenate(list(pieces(force)) + [jnp.zeros_like(force)], 0).astype(BF16)
-        back = mm(force, hot[...])
-        back = back[0:8] + back[8:16] + back[16:24]
-        for g in range(GROUP):
-            part_ref[g] += back[:, g * LANES:(g + 1) * LANES]
+        cols = pl.ds(pl.multiple_of(index * BLOCK, BLOCK), BLOCK)
+        r2 = mm(feature_ref[...], near_ref[:, cols])
+        dot = mm(feature_ref[...], along_ref[:, cols])
+        inv = lax.rsqrt(r2)
+        inv2 = inv * inv
+        w = inv * inv2
+        u = (w * inv2) * dot
+        sums = []
+        for value in (w, u):
+            high = value.astype(BF16)
+            low = (value - high.astype(F32)).astype(BF16)
+            sums.append(joined(mm(moment_ref[...], high) + mm(moment_ref[...], low)))
+        target = target_ref[:, cols]
+        by_w, by_u = [total - target * total[3:4, :] for total in sums]
+        force_ref[:, cols] = by_w - 3.0 * jnp.where(sub >= 4, pltpu.roll(by_u, 4, 0), 0.0)
         return carry
 
     lax.fori_loop(0, blocks, block, 0)
+    for g in range(GROUP):
+        tile = rank_ref[1, g:g + 1, :]
+        chosen = jnp.zeros((8, LANES), F32)
+        for at in range(tiles):
+            chosen = jnp.where(tile == at, force_ref[:, at * LANES:(at + 1) * LANES], chosen)
+        part_ref[g] = joined(mm(three_rows(chosen), hot[g]))
     row, col, core, zy, rc = place()
     await_greetings()
     for step in range(1, GROUP):
@@ -313,7 +319,7 @@
             jax.ShapeDtypeStruct((STARS, LANES), BF16),
             jax.ShapeDtypeStruct((32, STARS), BF16),
             jax.ShapeDtypeStruct(tiles, F32),
-            jax.ShapeDtypeStruct((GROUP, LANES), F32),
+            jax.ShapeDtypeStruct((2, GROUP, LANES), F32),
             jax.ShapeDtypeStruct((1,), jnp.int32),
         ),
         in_specs=[smem, smem] + [hbm] * 6,
@@ -327,7 +333,7 @@
             pltpu.SemaphoreType.DMA((2,)),
         ],
         compiler_params=pltpu.CompilerParams(
-            collective_id=0, has_side_effects=True, vmem_limit_bytes=8 * 2**20),
+            collective_id=0, has_side_effects=True, vmem_limit_bytes=56 * 2**20),
         name="gather_targets",
     )(active_index, active_count, position, velocity, accel_old, jerk_old,
       mass.reshape(TILES, LANES), elapsed.reshape(TILES, LANES))
@@ -340,7 +346,11 @@
             out_specs=vmem,
             scratch_shapes=[
                 pltpu.VMEM(tiles, F32),
-                pltpu.VMEM((BLOCK, SLOTS), BF16),
+                pltpu.VMEM((GROUP, LANES, LANES), BF16),
+                pltpu.VMEM((LANES, SIZES[at] * BLOCK), BF16),
+                pltpu.VMEM((LANES, SIZES[at] * BLOCK), BF16),
+                pltpu.VMEM((8, SIZES[at] * BLOCK), F32),
+                pltpu.VMEM((8, SIZES[at] * BLOCK), F32),
                 pltpu.VMEM((GROUP - 1, 8, LANES), F32),
                 pltpu.VMEM((GROUP - 1, 8, LANES), F32),
                 pltpu.VMEM((8, LANES), F32),

time: 53.1 us -> 44.6 us (0.84)
  local copies, waits for them, and re-layouts: 5.44 us -> 0 us
  Pallas kernels: 45 us -> 42.2 us
    unnamed x14 -> x0, local copies, waits for them, and re-layouts: 5.44 us -> none
    pallas_call x1, Pallas kernels: 21.9 us -> 19.2 us  [local(): lax.switch(choice[0], branches, active_count, features, moments, everyone...]
where the time goes in v4:
time: 44.6 us; the launch traced here: 44.4 us
  Pallas kernels  42.2 us (95%)
  between operations  1.93 us (4%)
    pallas_call x1, Pallas kernels, local(): pl.pallas_call(gather_kernel, out_shape=(jax.ShapeDtypeStruct((STARS, LAN...  22.4 us
    pallas_call x1, Pallas kernels, local(): lax.switch(choice[0], branches, active_count, features, moments, everyone...  19.2 us

profile of v4, /device:TPU:1, one launch (start us, length us, event | category | flops | bytes accessed | tf_op | source)
XLA Modules:
  0.0 44.4 jit_solution(4699537009747579404)
XLA Ops:
  1.3 22.4 %gather_targets.1 = (bf16[4096,128]{1,0:T(8,128)(2,1)S(1)}, bf16[32,4096]{1,0:T(8,128)(2,1)S(1)}, f32[16,8,128]{2,1,0:T(8,128)S(1)}, f32[2,16,128]{2,1,0:T(8,128)S(1)}, s32[1]{0:T(128)}) custom-call(s32[8]{0:T(128)} %index_ref.1, s32[1]{0:T(128)S(6)} %copy.13.count_ref, f32[3,4096]{1,0:T(4,128)} %pos_hbm.1, f32[3,4096]{1,0:T(4,128)} %vel_hbm.1, ...), custom_call_target="tpu_custom_call" | custom-call | tf_op jit(solution)/shard_map/gather_targets/pallas_call | solution.py:316
  24.3 19.5 %conditional.1 = (f32[8,128]{1,0:T(8,128)S(1)}) conditional(s32[]{:T(128)} %bitcast.2, (s32[1]{0:T(128)}, bf16[4096,128]{1,0:T(8,128)(2,1)S(1)}, bf16[32,4096]{1,0:T(8,128)(2,1)S(1)}, f32[16,8,128]{2,1,0:T(8,128)S(1)}, f32[2,16,128]{2,1,0:T(8,128)S(1)}) %tuple.16, (s32[1]{0:T(128)}, bf16[4096,128]{1,0:T(8,128)(2,1)S(1)}, ...), branch_computations={%region_0.0_spmd, %region_1.0_spmd, %region_2.0_spmd} | conditional | bytes 8 | solution.py:366
  24.3 19.2 %forces_3.1 = f32[8,128]{1,0:T(8,128)S(1)} custom-call(s32[1]{0:T(128)} %get-tuple-element.14.count_ref, bf16[4096,128]{1,0:T(8,128)(2,1)S(1)} %get-tuple-element.24.feature_ref, bf16[32,4096]{1,0:T(8,128)(2,1)S(1)} %get-tuple-element.36.moment_ref, f32[16,8,128]{2,1,0:T(8,128)S(1)} %get-tuple-element.37.all_ref, f32[2,16,128]{2,1,0:T(8,128)S(1)} %get-tuple-element.38.rank_ref), custom_call_target="tpu_custom_call" | custom-call | tf_op jit(solution)/shard_map/cond/branch_0_fun/forces_3/pallas_call | solution.py:366
  43.8 0.6 %finish.1 = (f32[3,8]{1,0:T(4,128)}, f32[3,8]{1,0:T(4,128)}) custom-call(f32[8,128]{1,0:T(8,128)S(1)} %get-tuple-element.61.force_ref), custom_call_target="tpu_custom_call" | custom-call | tf_op jit(solution)/shard_map/finish/pallas_call | solution.py:367

commit v5 on v4

--- a/solution.py
+++ b/solution.py
@@ -22,26 +22,34 @@
 def place():
     row = lax.axis_index("row")
     col = lax.axis_index("col")
-    core = lax.rem(col, 2)
-    return row, col, core, lax.div(col, 2), row * 2 + core
-
-
-def zy_peer(step):
-    row, col, core, zy, rc = place()
-    peer = lax.rem(zy + step, GROUP)
-    return peer, (row, peer * 2 + core)
-
-
-def rc_peer(step):
-    row, col, core, zy, rc = place()
-    peer = lax.rem(rc + step, GROUP)
-    return peer, (lax.div(peer, 2), zy * 2 + lax.rem(peer, 2))
+    z, y_lo, core = lax.div(col, 4), lax.rem(lax.div(col, 2), 2), lax.rem(col, 2)
+    return row, z, y_lo, core, z * 2 + core, row * 2 + y_lo
+
+
+def zc_peer(step):
+    row, z, y_lo, core, zc, xy = place()
+    peer = lax.rem(zc + step, GROUP)
+    return peer, (row, lax.div(peer, 2) * 4 + y_lo * 2 + lax.rem(peer, 2))
+
+
+def xy_peer(step):
+    row, z, y_lo, core, zc, xy = place()
+    peer = lax.rem(xy + step, GROUP)
+    return peer, (lax.div(peer, 2), z * 4 + lax.rem(peer, 2) * 2 + core)
+
+
+def ring(size, step):
+    return min(step % size, -step % size)
+
+
+ZC_STEPS = sorted(range(1, GROUP), key=lambda step: -ring(8, step // 2))
+XY_STEPS = sorted(range(1, GROUP), key=lambda step: -ring(4, step // 4) - ring(4, step))
 
 
 def greet():
     barrier = pltpu.get_barrier_semaphore()
-    for step in range(1, GROUP):
-        for peer in (zy_peer, rc_peer):
+    for peer, steps in ((zc_peer, ZC_STEPS), (xy_peer, XY_STEPS)):
+        for step in steps:
             pl.semaphore_signal(barrier, inc=1, device_id=peer(step)[1], device_id_type=MESH)
 
 
@@ -155,7 +163,7 @@
     ]
     for load in loads:
         load.start()
-    row, col, core, zy, rc = place()
+    row, z, y_lo, core, zc, xy = place()
     greet()
     for load in loads:
         load.wait()
@@ -176,11 +184,11 @@
             picked = jnp.where(away == -tile * LANES, stars[:, pl.ds(tile * LANES, LANES)], picked)
         value = jnp.sum(picked, axis=1, keepdims=True)
         value = jnp.where(sub == 3, jnp.where(slot < count_ref[0], 1.0, 0.0), value)
-        total = jnp.where(lane == zy * ACT + slot, value, total)
+        total = jnp.where(lane == zc * ACT + slot, value, total)
     mine[...] = total
     await_greetings()
-    for step in range(1, GROUP):
-        peer, device = zy_peer(step)
+    for step in ZC_STEPS:
+        peer, device = zc_peer(step)
         pltpu.make_async_remote_copy(
             src_ref=mine, dst_ref=near.at[step - 1],
             send_sem=send_sem.at[0], recv_sem=recv_sem.at[0],
@@ -194,11 +202,11 @@
     wait_bytes(near, recv_sem.at[0])
     for step in range(1, GROUP):
         total = total + near[step - 1]
-    all_ref[pl.ds(rc, 1)] = total[None]
-    for step in range(1, GROUP):
-        peer, device = rc_peer(step)
+    all_ref[pl.ds(xy, 1)] = total[None]
+    for step in XY_STEPS:
+        peer, device = xy_peer(step)
         pltpu.make_async_remote_copy(
-            src_ref=all_ref.at[rc], dst_ref=all_ref.at[rc],
+            src_ref=all_ref.at[xy], dst_ref=all_ref.at[xy],
             send_sem=send_sem.at[1], recv_sem=recv_sem.at[1],
             device_id=device, device_id_type=MESH).start()
     lax.fori_loop(TILES // 2, TILES, prepare, 0, unroll=2)
@@ -274,21 +282,21 @@
         for at in range(tiles):
             chosen = jnp.where(tile == at, force_ref[:, at * LANES:(at + 1) * LANES], chosen)
         part_ref[g] = joined(mm(three_rows(chosen), hot[g]))
-    row, col, core, zy, rc = place()
+    row, z, y_lo, core, zc, xy = place()
     await_greetings()
-    for step in range(1, GROUP):
-        peer, device = rc_peer(step)
+    for step in XY_STEPS:
+        peer, device = xy_peer(step)
         pltpu.make_async_remote_copy(
             src_ref=part_ref.at[peer], dst_ref=first.at[step - 1],
             send_sem=send_sem.at[0], recv_sem=recv_sem.at[0],
             device_id=device, device_id_type=MESH).start()
-    total = part_ref[rc]
+    total = part_ref[xy]
     wait_bytes(first, recv_sem.at[0])
     for step in range(1, GROUP):
         total = total + first[step - 1]
     summed[...] = total
-    for step in range(1, GROUP):
-        peer, device = zy_peer(step)
+    for step in ZC_STEPS:
+        peer, device = zc_peer(step)
         pltpu.make_async_remote_copy(
             src_ref=summed, dst_ref=second.at[step - 1],
             send_sem=send_sem.at[1], recv_sem=recv_sem.at[1],
@@ -296,7 +304,7 @@
     wait_bytes(second, recv_sem.at[1])
     for step in range(1, GROUP):
         total = total + second[step - 1]
-    mine = pltpu.roll(total, lax.rem(LANES - zy * ACT, LANES), 1)
+    mine = pltpu.roll(total, lax.rem(LANES - zc * ACT, LANES), 1)
     lane = lax.broadcasted_iota(jnp.int32, (8, LANES), 1)
     out_ref[...] = jnp.where(lane < count_ref[0], mine, 0.0)
     wait_bytes(first, send_sem.at[0])

time: 44.6 us -> 43.7 us (0.980)
  Pallas kernels: 42.2 us -> 41.4 us
    pallas_call x1, Pallas kernels: 22.4 us -> 20.4 us  [local(): pl.pallas_call(gather_kernel, out_shape=(jax.ShapeDtypeStruct((STARS, LAN...]
    pallas_call x1, Pallas kernels: 19.2 us -> 20.4 us  [local(): lax.switch(choice[0], branches, active_count, features, moments, everyone...]
where the time goes in v5:
time: 43.7 us; the launch traced here: 43.6 us
  Pallas kernels  41.4 us (95%)
  between operations  1.93 us (4%)
    pallas_call x1, Pallas kernels, local(): lax.switch(choice[0], branches, active_count, features, moments, everyone...  20.4 us
    pallas_call x1, Pallas kernels, local(): pl.pallas_call(gather_kernel, out_shape=(jax.ShapeDtypeStruct((STARS, LAN...  20.4 us

profile of v5, /device:TPU:1, one launch (start us, length us, event | category | flops | bytes accessed | tf_op | source)
XLA Modules:
  0.0 43.6 jit_solution(3563589062615238712)
XLA Ops:
  1.3 20.4 %gather_targets.1 = (bf16[4096,128]{1,0:T(8,128)(2,1)S(1)}, bf16[32,4096]{1,0:T(8,128)(2,1)S(1)}, f32[16,8,128]{2,1,0:T(8,128)S(1)}, f32[2,16,128]{2,1,0:T(8,128)S(1)}, s32[1]{0:T(128)}) custom-call(s32[8]{0:T(128)} %index_ref.1, s32[1]{0:T(128)S(6)} %copy.13.count_ref, f32[3,4096]{1,0:T(4,128)} %pos_hbm.1, f32[3,4096]{1,0:T(4,128)} %vel_hbm.1, ...), custom_call_target="tpu_custom_call" | custom-call | tf_op jit(solution)/shard_map/gather_targets/pallas_call | solution.py:324
  22.3 20.7 %conditional.1 = (f32[8,128]{1,0:T(8,128)S(1)}) conditional(s32[]{:T(128)} %bitcast.2, (s32[1]{0:T(128)}, bf16[4096,128]{1,0:T(8,128)(2,1)S(1)}, bf16[32,4096]{1,0:T(8,128)(2,1)S(1)}, f32[16,8,128]{2,1,0:T(8,128)S(1)}, f32[2,16,128]{2,1,0:T(8,128)S(1)}) %tuple.16, (s32[1]{0:T(128)}, bf16[4096,128]{1,0:T(8,128)(2,1)S(1)}, ...), branch_computations={%region_0.0_spmd, %region_1.0_spmd, %region_2.0_spmd} | conditional | bytes 8 | solution.py:374
  22.3 20.4 %forces_3.1 = f32[8,128]{1,0:T(8,128)S(1)} custom-call(s32[1]{0:T(128)} %get-tuple-element.14.count_ref, bf16[4096,128]{1,0:T(8,128)(2,1)S(1)} %get-tuple-element.24.feature_ref, bf16[32,4096]{1,0:T(8,128)(2,1)S(1)} %get-tuple-element.36.moment_ref, f32[16,8,128]{2,1,0:T(8,128)S(1)} %get-tuple-element.37.all_ref, f32[2,16,128]{2,1,0:T(8,128)S(1)} %get-tuple-element.38.rank_ref), custom_call_target="tpu_custom_call" | custom-call | tf_op jit(solution)/shard_map/cond/branch_0_fun/forces_3/pallas_call | solution.py:374
  43.0 0.6 %finish.1 = (f32[3,8]{1,0:T(4,128)}, f32[3,8]{1,0:T(4,128)}) custom-call(f32[8,128]{1,0:T(8,128)S(1)} %get-tuple-element.61.force_ref), custom_call_target="tpu_custom_call" | custom-call | tf_op jit(solution)/shard_map/finish/pallas_call | solution.py:375

commit v6 on v5

--- a/solution.py
+++ b/solution.py
@@ -16,7 +16,7 @@
 STARS = 4096
 TILES = STARS // LANES
 BLOCK = 256
-SIZES = (3, 4, 8)
+SIZES = ((3, 2), (4, 2), (8, 8))
 
 
 def place():
@@ -32,10 +32,11 @@
     return peer, (row, lax.div(peer, 2) * 4 + y_lo * 2 + lax.rem(peer, 2))
 
 
-def xy_peer(step):
+def xy_peer(offset):
     row, z, y_lo, core, zc, xy = place()
-    peer = lax.rem(xy + step, GROUP)
-    return peer, (lax.div(peer, 2), z * 4 + lax.rem(peer, 2) * 2 + core)
+    x = lax.rem(lax.div(row, 2) + offset[0], 4)
+    y = lax.rem(lax.rem(row, 2) * 2 + y_lo + offset[1], 4)
+    return x * 4 + y, (x * 2 + lax.div(y, 2), z * 4 + lax.rem(y, 2) * 2 + core)
 
 
 def ring(size, step):
@@ -43,7 +44,14 @@
 
 
 ZC_STEPS = sorted(range(1, GROUP), key=lambda step: -ring(8, step // 2))
-XY_STEPS = sorted(range(1, GROUP), key=lambda step: -ring(4, step // 4) - ring(4, step))
+XY_STEPS = sorted(((i // 4, i % 4) for i in range(1, GROUP)), key=lambda at: -ring(4, at[0]) - ring(4, at[1]))
+FAR = 9
+LAST_FAR = XY_STEPS[FAR - 1]
+
+
+def distances(tile, centre):
+    x, y = ((tile >> 2) - (centre >> 2)) & 3, ((tile & 3) - (centre & 3)) & 3
+    return jnp.minimum(x, 4 - x) + jnp.minimum(y, 4 - y), x * 4 + y
 
 
 def greet():
@@ -217,15 +225,27 @@
     after = lax.broadcasted_iota(jnp.int32, (LANES, LANES), 1)
     inside = mm(alive.astype(BF16), jnp.where(before < after, 1.0, 0.0).astype(BF16))
     sums = mm(alive.astype(BF16), jnp.ones((LANES, LANES), BF16))
-    earlier = jnp.where((after < before) & (after < GROUP), 1.0, 0.0)[0:GROUP, 0:GROUP]
-    ahead = mm(earlier.astype(BF16), sums.astype(BF16))
+    tile = lax.broadcasted_iota(jnp.int32, (GROUP, GROUP), 0)
+    other = lax.broadcasted_iota(jnp.int32, (GROUP, GROUP), 1)
+    (hops, step), (other_hops, other_step) = distances(tile, xy), distances(other, xy)
+    earlier = other_step - GROUP * other_hops < step - GROUP * hops
+    ahead = mm(jnp.where(earlier, 1.0, 0.0).astype(BF16), sums.astype(BF16))
+    hops, step = distances(other, tile)
+    last_hops, last_step = ring(4, LAST_FAR[0]) + ring(4, LAST_FAR[1]), LAST_FAR[0] * 4 + LAST_FAR[1]
+    far = step - GROUP * hops <= last_step - GROUP * last_hops
+    far = mm(jnp.where(far, 1.0, 0.0).astype(BF16), sums.astype(BF16))
     first = ahead - LANES * jnp.floor(ahead * (1.0 / LANES))
     lead = inside + first
     rank_ref[0] = jnp.where(alive > 0.0, lead - LANES * jnp.floor(lead * (1.0 / LANES)), -1.0)
     spot = lax.broadcasted_iota(jnp.int32, (GROUP, LANES), 1).astype(F32)
     rank_ref[1] = jnp.floor(ahead * (1.0 / LANES)) + jnp.where(spot < first, 1.0, 0.0)
-    live = (ahead + sums)[GROUP - 1, 0].astype(jnp.int32)
-    choice_ref[0] = sum((live > BLOCK * size).astype(jnp.int32) for size in SIZES[:-1])
+    live = jnp.max(ahead + sums, axis=0, keepdims=True)
+    far = jnp.max(far, axis=0, keepdims=True)
+    choice = jnp.full((1, LANES), len(SIZES) - 1.0, F32)
+    for at in reversed(range(len(SIZES) - 1)):
+        blocks, early = SIZES[at]
+        choice = jnp.where((live <= blocks * BLOCK) & (far <= early * BLOCK), float(at), choice)
+    choice_ref[0] = choice[0, 0].astype(jnp.int32)
     wait_bytes(near, send_sem.at[1])
 
 
@@ -237,7 +257,7 @@
     return rows[0:8] + rows[8:16] + rows[16:24]
 
 
-def force_kernel(blocks, count_ref, feature_ref, moment_ref, all_ref, rank_ref, out_ref,
+def force_kernel(blocks, early, count_ref, feature_ref, moment_ref, all_ref, rank_ref, out_ref,
                  part_ref, hot, near_ref, along_ref, target_ref, force_ref,
                  first, second, summed, send_sem, recv_sem):
     greet()
@@ -275,21 +295,41 @@
         force_ref[:, cols] = by_w - 3.0 * jnp.where(sub >= 4, pltpu.roll(by_u, 4, 0), 0.0)
         return carry
 
-    lax.fori_loop(0, blocks, block, 0)
-    for g in range(GROUP):
-        tile = rank_ref[1, g:g + 1, :]
+    def unpack(peer, done):
+        tile = rank_ref[1, pl.ds(peer, 1), :]
         chosen = jnp.zeros((8, LANES), F32)
-        for at in range(tiles):
+        for at in range(done * BLOCK // LANES):
             chosen = jnp.where(tile == at, force_ref[:, at * LANES:(at + 1) * LANES], chosen)
-        part_ref[g] = joined(mm(three_rows(chosen), hot[g]))
-    row, z, y_lo, core, zc, xy = place()
-    await_greetings()
-    for step in XY_STEPS:
-        peer, device = xy_peer(step)
+        part_ref[peer] = joined(mm(three_rows(chosen), hot[peer]))
+
+    def send(at, peer, device):
         pltpu.make_async_remote_copy(
-            src_ref=part_ref.at[peer], dst_ref=first.at[step - 1],
+            src_ref=part_ref.at[peer], dst_ref=first.at[at],
             send_sem=send_sem.at[0], recv_sem=recv_sem.at[0],
             device_id=device, device_id_type=MESH).start()
+
+    row, z, y_lo, core, zc, xy = place()
+    peers = [xy_peer(step) for step in XY_STEPS]
+
+    def send_far():
+        for peer, device in peers[:FAR]:
+            unpack(peer, early)
+        await_greetings()
+        for at in range(FAR):
+            send(at, *peers[at])
+
+    def step(index, carry):
+        pl.when(index == early)(send_far)
+        return block(index, carry)
+
+    lax.fori_loop(0, blocks, step, 0)
+    if early == blocks:
+        send_far()
+    for peer, device in peers[FAR:]:
+        unpack(peer, blocks)
+    for at in range(FAR, GROUP - 1):
+        send(at, *peers[at])
+    unpack(xy, blocks)
     total = part_ref[xy]
     wait_bytes(first, recv_sem.at[0])
     for step in range(1, GROUP):
@@ -348,17 +388,17 @@
 
     def forces(at):
         return pl.pallas_call(
-            functools.partial(force_kernel, SIZES[at]),
+            functools.partial(force_kernel, *SIZES[at]),
             out_shape=jax.ShapeDtypeStruct((8, LANES), F32),
             in_specs=[smem] + [vmem] * 4,
             out_specs=vmem,
             scratch_shapes=[
                 pltpu.VMEM(tiles, F32),
                 pltpu.VMEM((GROUP, LANES, LANES), BF16),
-                pltpu.VMEM((LANES, SIZES[at] * BLOCK), BF16),
-                pltpu.VMEM((LANES, SIZES[at] * BLOCK), BF16),
-                pltpu.VMEM((8, SIZES[at] * BLOCK), F32),
-                pltpu.VMEM((8, SIZES[at] * BLOCK), F32),
+                pltpu.VMEM((LANES, SIZES[at][0] * BLOCK), BF16),
+                pltpu.VMEM((LANES, SIZES[at][0] * BLOCK), BF16),
+                pltpu.VMEM((8, SIZES[at][0] * BLOCK), F32),
+                pltpu.VMEM((8, SIZES[at][0] * BLOCK), F32),
                 pltpu.VMEM((GROUP - 1, 8, LANES), F32),
                 pltpu.VMEM((GROUP - 1, 8, LANES), F32),
                 pltpu.VMEM((8, LANES), F32),
@@ -367,7 +407,7 @@
             ],
             compiler_params=pltpu.CompilerParams(
                 collective_id=1 + at, has_side_effects=True, vmem_limit_bytes=24 * 2**20),
-            name="forces_%d" % SIZES[at],
+            name="forces_%d" % SIZES[at][0],
         )
 
     branches = [forces(at) for at in range(len(SIZES))]

time: 43.7 us -> 42.7 us (0.977)
  Pallas kernels: 41.4 us -> 40.4 us
    pallas_call x1, Pallas kernels: 20.4 us -> 19.5 us  [local(): lax.switch(choice[0], branches, active_count, features, moments, everyone...]
where the time goes in v6:
time: 42.7 us; the launch traced here: 42.6 us
  Pallas kernels  40.4 us (95%)
  between operations  1.93 us (5%)
    pallas_call x1, Pallas kernels, local(): pl.pallas_call(gather_kernel, out_shape=(jax.ShapeDtypeStruct((STARS, LAN...  20.3 us
    pallas_call x1, Pallas kernels, local(): lax.switch(choice[0], branches, active_count, features, moments, everyone...  19.5 us

profile of v6, /device:TPU:1, one launch (start us, length us, event | category | flops | bytes accessed | tf_op | source)
XLA Modules:
  0.0 42.6 jit_solution(9128182529940141200)
XLA Ops:
  1.3 20.3 %gather_targets.1 = (bf16[4096,128]{1,0:T(8,128)(2,1)S(1)}, bf16[32,4096]{1,0:T(8,128)(2,1)S(1)}, f32[16,8,128]{2,1,0:T(8,128)S(1)}, f32[2,16,128]{2,1,0:T(8,128)S(1)}, s32[1]{0:T(128)}) custom-call(s32[8]{0:T(128)} %index_ref.1, s32[1]{0:T(128)S(6)} %copy.13.count_ref, f32[3,4096]{1,0:T(4,128)} %pos_hbm.1, f32[3,4096]{1,0:T(4,128)} %vel_hbm.1, ...), custom_call_target="tpu_custom_call" | custom-call | tf_op jit(solution)/shard_map/gather_targets/pallas_call | solution.py:364
  22.3 19.7 %conditional.1 = (f32[8,128]{1,0:T(8,128)S(1)}) conditional(s32[]{:T(128)} %bitcast.2, (s32[1]{0:T(128)}, bf16[4096,128]{1,0:T(8,128)(2,1)S(1)}, bf16[32,4096]{1,0:T(8,128)(2,1)S(1)}, f32[16,8,128]{2,1,0:T(8,128)S(1)}, f32[2,16,128]{2,1,0:T(8,128)S(1)}) %tuple.16, (s32[1]{0:T(128)}, bf16[4096,128]{1,0:T(8,128)(2,1)S(1)}, ...), branch_computations={%region_0.0_spmd, %region_1.0_spmd, %region_2.0_spmd} | conditional | bytes 8 | solution.py:414
  22.3 19.5 %forces_3.1 = f32[8,128]{1,0:T(8,128)S(1)} custom-call(s32[1]{0:T(128)} %get-tuple-element.14.count_ref, bf16[4096,128]{1,0:T(8,128)(2,1)S(1)} %get-tuple-element.24.feature_ref, bf16[32,4096]{1,0:T(8,128)(2,1)S(1)} %get-tuple-element.36.moment_ref, f32[16,8,128]{2,1,0:T(8,128)S(1)} %get-tuple-element.37.all_ref, f32[2,16,128]{2,1,0:T(8,128)S(1)} %get-tuple-element.38.rank_ref), custom_call_target="tpu_custom_call" | custom-call | tf_op jit(solution)/shard_map/cond/branch_0_fun/forces_3/pallas_call | solution.py:414
  42.0 0.6 %finish.1 = (f32[3,8]{1,0:T(4,128)}, f32[3,8]{1,0:T(4,128)}) custom-call(f32[8,128]{1,0:T(8,128)S(1)} %get-tuple-element.61.force_ref), custom_call_target="tpu_custom_call" | custom-call | tf_op jit(solution)/shard_map/finish/pallas_call | solution.py:415

commit v7 on v3

v7 whole, which is shorter than its diff:
```python
import jax
import jax.numpy as jnp
from jax import lax
from jax.experimental import pallas as pl
from jax.experimental.pallas import tpu as pltpu
from jax.sharding import PartitionSpec as P

SOFTENING = 0.0025
MESH = pl.DeviceIdType.MESH
F32, BF16 = jnp.float32, jnp.bfloat16
LANES = 128
GROUP = 16
ACT = 8
STARS = 4096
TILES = STARS // LANES
BLOCK = 256
MIDDLE = 512
ROOM = 896
SLOTS = GROUP * LANES


def ring(size, step):
    return min(step % size, -step % size)


def hops(step):
    return ring(4, step[0]) + ring(4, step[1])


ZC_STEPS = sorted(range(1, GROUP), key=lambda step: -ring(8, step // 2))
XY_STEPS = sorted(((i // 4, i % 4) for i in range(GROUP)), key=lambda step: (2, 3, 4, 1, 0).index(hops(step)))
START = sum(hops(step) == 2 for step in XY_STEPS)
EARLY = sum(hops(step) >= 2 for step in XY_STEPS)
NEAR_FIRST = sorted(range(GROUP - 1), key=lambda at: hops(XY_STEPS[at]))
FAR_FIRST = NEAR_FIRST[::-1]


def place():
    row = lax.axis_index("row")
    col = lax.axis_index("col")
    z, y_lo, core = col >> 2, (col >> 1) & 1, col & 1
    return row, z, y_lo, core, z * 2 + core, row * 2 + y_lo


def zc_peers():
    row, z, y_lo, core, zc, xy = place()
    peers = []
    for step in ZC_STEPS:
        peer = (zc + step) & (GROUP - 1)
        peers.append((peer, (row, (peer >> 1) * 4 + y_lo * 2 + (peer & 1))))
    return peers


def xy_peers():
    row, z, y_lo, core, zc, xy = place()
    rows = [((row >> 1) + step) & 3 for step in range(4)]
    columns = [((row & 1) * 2 + y_lo + step) & 3 for step in range(4)]
    peers = []
    for step in XY_STEPS:
        x, y = rows[step[0]], columns[step[1]]
        peers.append((x * 4 + y, (x * 2 + (y >> 1), z * 4 + (y & 1) * 2 + core)))
    return peers


def greet():
    barrier = pltpu.get_barrier_semaphore()
    for peer, device in zc_peers() + xy_peers()[:-1]:
        pl.semaphore_signal(barrier, inc=1, device_id=device, device_id_type=MESH)


def await_greetings():
    pl.semaphore_wait(pltpu.get_barrier_semaphore(), 2 * (GROUP - 1))


def wait_bytes(ref, sem):
    pltpu.make_async_copy(ref, ref, sem).wait()


def send(src, dst, sent, landed, device):
    pltpu.make_async_remote_copy(
        src_ref=src, dst_ref=dst, send_sem=sent, recv_sem=landed,
        device_id=device, device_id_type=MESH).start()


def mm(a, b):
    return jnp.dot(a, b, preferred_element_type=F32)


def mm_t(a, b):
    return lax.dot_general(a, b, (((1,), (1,)), ((), ())), preferred_element_type=F32)


def pieces(value):
    first = value.astype(BF16).astype(F32)
    rest = value - first
    second = rest.astype(BF16).astype(F32)
    return first, second, rest - second


def coordinates(group):
    coarse = jnp.floor(group * 16.0 + 0.5) * 0.0625
    return coarse, pieces(group - coarse)


def scalars(group, coarse, shift):
    sub = lax.broadcasted_iota(jnp.int32, group.shape, 0)
    upper = sub < 3

    def pair(exact, whole):
        exact = jnp.sum(jnp.where(upper, exact, 0.0), axis=0, keepdims=True)
        whole = jnp.sum(jnp.where(upper, whole, 0.0), axis=0, keepdims=True)
        high = exact.astype(BF16).astype(F32)
        return (high, exact - high) + pieces(whole)

    fine = group - coarse
    vel, vel_coarse = pltpu.roll(group, 4, 0), pltpu.roll(coarse, 4, 0)
    square = pair(coarse * coarse, fine * (group + coarse) + jnp.where(sub == 0, shift, 0.0))
    cross = pair(coarse * vel_coarse, fine * vel + coarse * (vel - vel_coarse))
    return square, cross


def stack(rows, shape):
    sub = lax.broadcasted_iota(jnp.int32, shape, 0)
    total = jnp.zeros(shape, F32)
    for at, row in enumerate(rows):
        total = jnp.where(sub == at, row, total)
    return total


def source_features(group):
    coarse, (one, two, three) = coordinates(group)
    square, cross = scalars(group, coarse, 0.0)
    exact = stack(square[0:2] + (1.0, 1.0) + cross[0:2] + (1.0, 1.0), group.shape)
    rest = stack(square[2:5] + (1.0,) + cross[2:5] + (1.0,), group.shape)
    more = stack((1.0, 1.0, 0.0, 0.0, 1.0, 1.0, 0.0, 0.0), group.shape)
    none = jnp.zeros_like(group)
    return [exact, coarse, rest, more, coarse, coarse, coarse, one, two, three, one, one, two, two, none, none]


def target_features(group):
    coarse, (one, two, three) = coordinates(group)
    square, cross = scalars(group, coarse, SOFTENING)
    sub = lax.broadcasted_iota(jnp.int32, group.shape, 0)
    none = jnp.zeros_like(group)

    def tail(scalar, at):
        pad, rest = (0.0,) * at, (0.0,) * (4 - at)
        exact = stack(pad + (1.0, 1.0) + scalar[0:2] + rest, group.shape)
        fine = stack(pad + (1.0, 1.0, 1.0) + scalar[2:3] + rest, group.shape)
        more = stack(pad + scalar[3:5] + (0.0, 0.0) + rest, group.shape)
        return exact, fine, more

    def weights(change, scalar, at):
        exact, fine, more = tail(scalar, at)
        c, o, t, h = change(coarse), change(one), change(two), change(three)
        rows = [exact, c, fine, more, o, t, h, c, c, c, o, t, o, t, none, none]
        return jnp.concatenate(rows, 0).astype(BF16)

    near = weights(lambda v: jnp.where(sub < 3, -2.0 * v, 0.0), square, 0)
    along = weights(lambda v: -pltpu.roll(v, 4, 0), cross, 4)
    return near, along


def prepare_tile(tile, stars, mass_ref, feature_ref, moment_ref):
    cols = pl.ds(pl.multiple_of(tile * LANES, LANES), LANES)
    group = stars[:, cols]
    rows = jnp.concatenate(source_features(group), 0)
    feature_ref[cols, :] = rows.T.astype(BF16)
    sub = lax.broadcasted_iota(jnp.int32, group.shape, 0)
    moment = mass_ref[pl.ds(tile, 1), :] * jnp.where(sub == 3, 1.0, group)
    one, two, three = pieces(moment)
    moment_ref[:, cols] = jnp.concatenate([one, two, three, jnp.zeros_like(one)], 0).astype(BF16)


def three_rows(group):
    return jnp.concatenate(list(pieces(group)) + [jnp.zeros_like(group)], 0).astype(BF16)


def joined(rows):
    return rows[0:8] + rows[8:16] + rows[16:24]


def places(alive, start):
    before = lax.broadcasted_iota(jnp.int32, (LANES, LANES), 0)
    after = lax.broadcasted_iota(jnp.int32, (LANES, LANES), 1)
    tile = lax.broadcasted_iota(jnp.int32, (GROUP, GROUP), 0)
    other = lax.broadcasted_iota(jnp.int32, (GROUP, GROUP), 1)
    alive_b = alive.astype(BF16)
    inside = mm(alive_b, jnp.where(before < after, 1.0, 0.0).astype(BF16))
    sums = mm(alive_b, jnp.ones((LANES, LANES), BF16))
    ahead = mm(jnp.where(other < tile, 1.0, 0.0).astype(BF16), sums.astype(BF16))
    if start:
        late = lax.broadcasted_iota(jnp.int32, (GROUP, LANES), 0) >= start
        ahead = ahead + jnp.where(late, jnp.maximum(BLOCK - ahead[start:start + 1, :], 0.0), 0.0)
    first = ahead - LANES * jnp.floor(ahead * (1.0 / LANES))
    lead = inside + first
    lane = jnp.where(alive > 0.0, lead - LANES * jnp.floor(lead * (1.0 / LANES)), -1.0)
    spot = lax.broadcasted_iota(jnp.int32, (GROUP, LANES), 1).astype(F32)
    return lane, jnp.floor(ahead * (1.0 / LANES)) + jnp.where(spot < first, 1.0, 0.0)


def pack(at, group, lane, tile, hot, packed):
    spot = lax.broadcasted_iota(jnp.int32, (LANES, LANES), 0).astype(F32)
    hot[at] = jnp.where(spot == lane[at:at + 1, :], 1.0, 0.0).astype(BF16)
    chosen = joined(mm_t(three_rows(group), hot[at]))
    return [old + jnp.where(tile[at:at + 1, :] == number, chosen, 0.0) for number, old in enumerate(packed)]


def unpack(at, tile, numbers, hot, force_ref):
    chosen = jnp.zeros((8, LANES), F32)
    for number in numbers:
        chosen = jnp.where(tile == number, force_ref[:, number * LANES:(number + 1) * LANES], chosen)
    return joined(mm(three_rows(chosen), hot[at]))


def weigh(number, packed, target_ref, near_ref, along_ref):
    sub = lax.broadcasted_iota(jnp.int32, (8, LANES), 0)
    cols = pl.ds(number * LANES, LANES)
    target = jnp.where((sub == 3) | (sub == 7), 0.0, packed)
    target_ref[:, cols] = target
    near_ref[:, cols], along_ref[:, cols] = target_features(target)


def pair_weights(r2, dot):
    inv = lax.rsqrt(r2)
    inv2 = inv * inv
    w = inv * inv2
    out = []
    for value in (w, (w * inv2) * dot):
        high = value.astype(BF16)
        out.append((high, (value - high.astype(F32)).astype(BF16)))
    return out


def force_of(by_w, by_u, target):
    sub = lax.broadcasted_iota(jnp.int32, target.shape, 0)
    by_w, by_u = by_w - target * by_w[3:4, :], by_u - target * by_u[3:4, :]
    return by_w - 3.0 * jnp.where(sub >= 4, pltpu.roll(by_u, 4, 0), 0.0)


def force_block(lead, feature_ref, moment_ref, near_ref, along_ref, target_ref, force_ref):
    cols = pl.ds(pl.multiple_of(lead, LANES), BLOCK)
    r2 = mm(feature_ref[...], near_ref[:, cols])
    dot = mm(feature_ref[...], along_ref[:, cols])
    sums = [joined(mm(moment_ref[...], high) + mm(moment_ref[...], low)) for high, low in pair_weights(r2, dot)]
    force_ref[:, cols] = force_of(*sums, target_ref[:, cols])


def force_half_block(lead, feature_ref, moment_ref, near_ref, along_ref, target_ref, force_ref):
    cols = pl.ds(lead, LANES)
    both = mm(feature_ref[...], jnp.concatenate([near_ref[:, cols], along_ref[:, cols]], 1))
    sums = []
    for high, low in pair_weights(both[:, :LANES], both[:, LANES:]):
        total = mm(moment_ref[...], jnp.concatenate([high, low], 1))
        sums.append(joined(total[:, :LANES] + total[:, LANES:]))
    force_ref[:, cols] = force_of(*sums, target_ref[:, cols])


def last_stage(total, summed, second, send_sem, recv_sem):
    summed[...] = total
    for at, (peer, device) in enumerate(zc_peers()):
        send(summed, second.at[at], send_sem, recv_sem, device)


def last_sum(total, count_ref, second, recv_sem):
    wait_bytes(second, recv_sem)
    for at in range(GROUP - 1):
        total = total + second[at]
    row, z, y_lo, core, zc, xy = place()
    mine = pltpu.roll(total, (LANES - zc * ACT) & (LANES - 1), 1)
    lane = lax.broadcasted_iota(jnp.int32, (8, LANES), 1)
    return jnp.where(lane < count_ref[0], mine, 0.0)


def overfull(all_ref):
    alive = jnp.concatenate([all_ref[g, 3:4, :] for g in range(GROUP)], 0).astype(BF16)
    sums = mm(alive, jnp.ones((LANES, LANES), BF16)).astype(BF16)
    centre = lax.broadcasted_iota(jnp.int32, (GROUP, GROUP), 0)
    tile = lax.broadcasted_iota(jnp.int32, (GROUP, GROUP), 1)
    x, y = ((tile >> 2) - (centre >> 2)) & 3, ((tile & 3) - (centre & 3)) & 3
    away = jnp.minimum(x, 4 - x) + jnp.minimum(y, 4 - y)
    begun, far, near = [
        mm(jnp.where(of, 1.0, 0.0).astype(BF16), sums) for of in (away == 2, away > 2, away < 2)]
    early = jnp.maximum(begun, float(BLOCK)) + far
    over = (early > MIDDLE + LANES) | (early + near > ROOM)
    return jnp.max(jnp.where(over, 1.0, 0.0), axis=0, keepdims=True)[0, 0].astype(jnp.int32)


def fast_kernel(index_ref, count_ref, pos_hbm, vel_hbm, acc_hbm, jerk_hbm, mass_hbm, elapsed_hbm,
                out_ref, stars, all_ref, choice_ref,
                pos_ref, vel_ref, acc_ref, jerk_ref, mass_ref, elapsed_ref,
                feature_ref, moment_ref, mine, landed, tile_ref, hot, near_ref, along_ref, target_ref,
                force_ref, part_ref, first, second, summed, load_sem, send_sem, recv_sem):
    loads = [
        pltpu.make_async_copy(src, dst, load_sem.at[at])
        for at, (src, dst) in enumerate((
            (pos_hbm, pos_ref), (vel_hbm, vel_ref), (acc_hbm, acc_ref), (jerk_hbm, jerk_ref),
            (mass_hbm, mass_ref), (elapsed_hbm, elapsed_ref)))
    ]
    for load in loads:
        load.start()
    greet()
    for load in loads:
        load.wait()
    row, z, y_lo, core, zc, xy = place()
    stars[...] = jnp.zeros_like(stars)
    for tile in range(TILES):
        cols = pl.ds(tile * LANES, LANES)
        dt = elapsed_ref[tile:tile + 1, :]
        vel, acc, jerk = vel_ref[:, cols], acc_ref[:, cols], jerk_ref[:, cols]
        stars[0:3, cols] = pos_ref[:, cols] + dt * (vel + dt * (0.5 * acc + dt * (jerk * (1.0 / 6.0))))
        stars[4:7, cols] = vel + dt * (acc + dt * (0.5 * jerk))
    lane = lax.broadcasted_iota(jnp.int32, (8, LANES), 1)
    sub = lax.broadcasted_iota(jnp.int32, (8, LANES), 0)
    total = jnp.zeros((8, LANES), F32)
    for slot in range(ACT):
        away = lane - index_ref[slot]
        picked = jnp.zeros((8, LANES), F32)
        for tile in range(TILES):
            picked = jnp.where(away == -tile * LANES, stars[:, pl.ds(tile * LANES, LANES)], picked)
        value = jnp.sum(picked, axis=1, keepdims=True)
        value = jnp.where(sub == 3, jnp.where(slot < count_ref[0], 1.0, 0.0), value)
        total = jnp.where(lane == zc * ACT + slot, value, total)
    mine[...] = total
    await_greetings()
    for at, (peer, device) in enumerate(zc_peers()):
        send(mine, landed.at[at], send_sem.at[0], recv_sem.at[0], device)

    def prepare(tile, carry):
        prepare_tile(tile, stars, mass_ref, feature_ref, moment_ref)
        return carry

    lax.fori_loop(0, TILES // 2, prepare, 0, unroll=2)
    wait_bytes(landed, recv_sem.at[0])
    for at in range(GROUP - 1):
        total = total + landed[at]
    all_ref[pl.ds(xy, 1)] = total[None]
    peers = xy_peers()
    for at in FAR_FIRST:
        far = 2 if START <= at < EARLY else 1
        send(all_ref.at[xy], all_ref.at[xy], send_sem.at[1], recv_sem.at[far], peers[at][1])
    lax.fori_loop(TILES // 2, TILES, prepare, 0, unroll=2)

    wait_bytes(landed.at[pl.ds(0, GROUP - 1 - EARLY + START)], recv_sem.at[1])
    none = jnp.zeros((1, LANES), F32)
    numbers = ROOM // LANES
    spots, tiles = places(jnp.concatenate(
        [all_ref[peer, 3:4, :] for peer, device in peers[:START]] + [none] * (GROUP - START), 0), START)
    packed = [jnp.zeros((8, LANES), F32)] * numbers
    for at in range(START):
        packed = pack(at, all_ref[peers[at][0]], spots, tiles, hot, packed)
    for number in range(2):
        weigh(number, packed[number], target_ref, near_ref, along_ref)
    for number in range(2, numbers):
        target_ref[:, number * LANES:(number + 1) * LANES] = packed[number]

    def pack_rest():
        wait_bytes(landed.at[pl.ds(0, EARLY - START)], recv_sem.at[2])
        spots, tiles = places(jnp.concatenate([all_ref[peer, 3:4, :] for peer, device in peers], 0), START)
        tile_ref[...] = tiles
        packed = [target_ref[:, number * LANES:(number + 1) * LANES] for number in range(numbers)]
        for at in range(START, GROUP):
            packed = pack(at, all_ref[peers[at][0]], spots, tiles, hot, packed)
        for number in range(2, numbers):
            weigh(number, packed[number], target_ref, near_ref, along_ref)

    refs = (feature_ref, moment_ref, near_ref, along_ref, target_ref, force_ref)

    def send_early():
        force_half_block(MIDDLE, *refs)
        for at in range(EARLY):
            part_ref[at] = unpack(at, tile_ref[at:at + 1, :], range((MIDDLE + LANES) // LANES), hot, force_ref)
        for at in FAR_FIRST:
            if at < EARLY:
                send(part_ref.at[at], first.at[at], send_sem.at[2], recv_sem.at[3], peers[at][1])

    def step(index, carry):
        pl.when(index == 1)(pack_rest)
        pl.when(index == 2)(send_early)
        force_block(index * BLOCK + (index >> 1) * LANES, *refs)
        return carry

    lax.fori_loop(0, 3, step, 0)
    for at in range(EARLY, GROUP):
        part_ref[at] = unpack(at, tile_ref[at:at + 1, :], range(2, numbers), hot, force_ref)
        if at < GROUP - 1:
            send(part_ref.at[at], first.at[at], send_sem.at[2], recv_sem.at[3], peers[at][1])
    total = part_ref[GROUP - 1]
    wait_bytes(first, recv_sem.at[3])
    for at in range(GROUP - 1):
        total = total + first[at]
    last_stage(total, summed, second, send_sem.at[3], recv_sem.at[4])
    choice_ref[0] = overfull(all_ref)
    out_ref[...] = last_sum(total, count_ref, second, recv_sem.at[4])
    for at in range(4):
        wait_bytes(landed, send_sem.at[at])


def general_kernel(count_ref, mass_ref, stars, all_ref, out_ref,
                   feature_ref, moment_ref, tile_ref, hot, near_ref, along_ref, target_ref,
                   force_ref, part_ref, first, second, summed, send_sem, recv_sem):
    greet()

    def prepare(tile, carry):
        prepare_tile(tile, stars, mass_ref, feature_ref, moment_ref)
        return carry

    lax.fori_loop(0, TILES, prepare, 0)
    numbers = SLOTS // LANES
    spots, tiles = places(jnp.concatenate([all_ref[g, 3:4, :] for g in range(GROUP)], 0), 0)
    tile_ref[...] = tiles
    packed = [jnp.zeros((8, LANES), F32)] * numbers
    for at in range(GROUP):
        packed = pack(at, all_ref[at], spots, tiles, hot, packed)
    for number in range(numbers):
        weigh(number, packed[number], target_ref, near_ref, along_ref)

    def step(index, carry):
        force_block(index * BLOCK, feature_ref, moment_ref, near_ref, along_ref, target_ref, force_ref)
        return carry

    lax.fori_loop(0, SLOTS // BLOCK, step, 0)
    for at in range(GROUP):
        part_ref[at] = unpack(at, tile_ref[at:at + 1, :], range(numbers), hot, force_ref)
    await_greetings()
    peers = xy_peers()
    for at in FAR_FIRST:
        peer, device = peers[at]
        send(part_ref.at[peer], first.at[at], send_sem.at[0], recv_sem.at[0], device)
    total = part_ref[peers[-1][0]]
    wait_bytes(first, recv_sem.at[0])
    for at in range(GROUP - 1):
        total = total + first[at]
    last_stage(total, summed, second, send_sem.at[1], recv_sem.at[1])
    out_ref[...] = last_sum(total, count_ref, second, recv_sem.at[1])
    for at in range(2):
        wait_bytes(first, send_sem.at[at])


def finish_kernel(force_ref, accel_ref, jerk_ref):
    accel_ref[...] = force_ref[0:3, 0:ACT]
    jerk_ref[...] = force_ref[4:7, 0:ACT]


def force_scratch(room):
    return [
        pltpu.VMEM((GROUP, LANES), F32),
        pltpu.VMEM((GROUP, LANES, LANES), BF16),
        pltpu.VMEM((LANES, room), BF16),
        pltpu.VMEM((LANES, room), BF16),
        pltpu.VMEM((8, room), F32),
        pltpu.VMEM((8, room), F32),
        pltpu.VMEM((GROUP, 8, LANES), F32),
        pltpu.VMEM((GROUP - 1, 8, LANES), F32),
        pltpu.VMEM((GROUP - 1, 8, LANES), F32),
        pltpu.VMEM((8, LANES), F32),
    ]


def local(position, velocity, accel_old, jerk_old, mass, elapsed, active_index, active_count):
    vmem = pl.BlockSpec(memory_space=pltpu.VMEM)
    smem = pl.BlockSpec(memory_space=pltpu.SMEM)
    hbm = pl.BlockSpec(memory_space=pltpu.HBM)
    star_scratch = [pltpu.VMEM((STARS, LANES), BF16), pltpu.VMEM((32, STARS), BF16)]
    mass = mass.reshape(TILES, LANES)
    mine, stars, everyone, choice = pl.pallas_call(
        fast_kernel,
        out_shape=(
            jax.ShapeDtypeStruct((8, LANES), F32),
            jax.ShapeDtypeStruct((8, STARS), F32),
            jax.ShapeDtypeStruct((GROUP, 8, LANES), F32),
            jax.ShapeDtypeStruct((1,), jnp.int32),
        ),
        in_specs=[smem, smem] + [hbm] * 6,
        out_specs=(vmem,) * 3 + (smem,),
        scratch_shapes=[pltpu.VMEM((3, STARS), F32)] * 4 + [pltpu.VMEM((TILES, LANES), F32)] * 2
        + star_scratch + [
            pltpu.VMEM((8, LANES), F32),
            pltpu.VMEM((GROUP - 1, 8, LANES), F32),
        ] + force_scratch(ROOM) + [
            pltpu.SemaphoreType.DMA((6,)),
            pltpu.SemaphoreType.DMA((4,)),
            pltpu.SemaphoreType.DMA((5,)),
        ],
        compiler_params=pltpu.CompilerParams(
            collective_id=0, has_side_effects=True, vmem_limit_bytes=56 * 2**20),
        name="fast",
    )(active_index, active_count, position, velocity, accel_old, jerk_old, mass, elapsed.reshape(TILES, LANES))

    def general():
        return pl.pallas_call(
            general_kernel,
            out_shape=jax.ShapeDtypeStruct((8, LANES), F32),
            in_specs=[smem] + [vmem] * 3,
            out_specs=vmem,
            scratch_shapes=star_scratch + force_scratch(SLOTS) + [
                pltpu.SemaphoreType.DMA((2,)),
                pltpu.SemaphoreType.DMA((2,)),
            ],
            compiler_params=pltpu.CompilerParams(
                collective_id=1, has_side_effects=True, vmem_limit_bytes=32 * 2**20),
            name="general",
        )(active_count, mass, stars, everyone)

    mine = lax.cond(choice[0] > 0, general, lambda: mine)
    return pl.pallas_call(
        finish_kernel,
        out_shape=(jax.ShapeDtypeStruct((3, ACT), F32), jax.ShapeDtypeStruct((3, ACT), F32)),
        in_specs=[vmem],
        out_specs=(vmem, vmem),
        name="finish",
    )(mine)


def solution(mesh):
    split = P(None, ("row", "col"))
    flat = P(("row", "col"))
    return jax.shard_map(
        local,
        mesh=mesh,
        in_specs=(split, split, split, split, flat, flat, flat, flat),
        out_specs=(split, split),
        check_vma=False,
    )
```

time: 53.1 us -> 43.5 us (0.82)
  local copies, waits for them, and re-layouts: 5.44 us -> 0.01 us
  Pallas kernels: 45 us -> 41.4 us
    unnamed x14 -> x2, local copies, waits for them, and re-layouts: 5.44 us -> 0.01 us
    pallas_call x2 -> x1, Pallas kernels: 44.4 us -> 40.8 us  [local(): pl.pallas_call(fast_kernel, out_shape=(jax.ShapeDtypeStruct((8, LANES), F...]
where the time goes in v7:
time: 43.5 us; the launch traced here: 43.3 us
  Pallas kernels  41.4 us (95%)
  between operations  1.92 us (4%)
    pallas_call x1, Pallas kernels, local(): pl.pallas_call(fast_kernel, out_shape=(jax.ShapeDtypeStruct((8, LANES), F...  40.8 us

profile of v7, /device:TPU:1, one launch (start us, length us, event | category | flops | bytes accessed | tf_op | source)
XLA Modules:
  0.0 43.3 jit_solution(15772494745264639399)
XLA Ops:
  1.3 0.0 copy-start
  1.3 40.8 %fast.1 = (f32[8,128]{1,0:T(8,128)S(1)}, f32[8,4096]{1,0:T(8,128)S(1)}, f32[16,8,128]{2,1,0:T(8,128)S(1)}, s32[1]{0:T(128)}) custom-call(s32[8]{0:T(128)} %index_ref.1, s32[1]{0:T(128)S(6)} %copy.12.count_ref, f32[3,4096]{1,0:T(4,128)} %pos_hbm.1, f32[3,4096]{1,0:T(4,128)} %vel_hbm.1, f32[3,4096]{1,0:T(4,128)} %acc_hbm.1, f32[3,4096]{1,0:T(4,128)} %jerk_hbm.1, ...), custom_call_target="tpu_custom_call" | custom-call | tf_op jit(solution)/shard_map/fast/pallas_call | solution.py:466
  42.7 0.0 copy-done
  42.7 0.6 %finish.1 = (f32[3,8]{1,0:T(4,128)}, f32[3,8]{1,0:T(4,128)}) custom-call(f32[8,128]{1,0:T(8,128)S(1)} %get-tuple-element.26.force_ref), custom_call_target="tpu_custom_call" | custom-call | tf_op jit(solution)/shard_map/finish/pallas_call | solution.py:506
  (1 shorter events, 0.0 us)
Async XLA Ops:
  1.3 41.4 %copy-start = (f32[4096]{0:T(1024)S(1)}, f32[4096]{0:T(1024)}, u32[]{:S(2)}) copy-start(f32[4096]{0:T(1024)} %param.14) | copy-start | bytes 49156

commit v8 on v6

--- a/solution.py
+++ b/solution.py
@@ -19,26 +19,6 @@
 SIZES = ((3, 2), (4, 2), (8, 8))
 
 
-def place():
-    row = lax.axis_index("row")
-    col = lax.axis_index("col")
-    z, y_lo, core = lax.div(col, 4), lax.rem(lax.div(col, 2), 2), lax.rem(col, 2)
-    return row, z, y_lo, core, z * 2 + core, row * 2 + y_lo
-
-
-def zc_peer(step):
-    row, z, y_lo, core, zc, xy = place()
-    peer = lax.rem(zc + step, GROUP)
-    return peer, (row, lax.div(peer, 2) * 4 + y_lo * 2 + lax.rem(peer, 2))
-
-
-def xy_peer(offset):
-    row, z, y_lo, core, zc, xy = place()
-    x = lax.rem(lax.div(row, 2) + offset[0], 4)
-    y = lax.rem(lax.rem(row, 2) * 2 + y_lo + offset[1], 4)
-    return x * 4 + y, (x * 2 + lax.div(y, 2), z * 4 + lax.rem(y, 2) * 2 + core)
-
-
 def ring(size, step):
     return min(step % size, -step % size)
 
@@ -49,6 +29,33 @@
 LAST_FAR = XY_STEPS[FAR - 1]
 
 
+def place():
+    row = lax.axis_index("row")
+    col = lax.axis_index("col")
+    z, y_lo, core = col >> 2, (col >> 1) & 1, col & 1
+    return row, z, y_lo, core, z * 2 + core, row * 2 + y_lo
+
+
+def zc_peers():
+    row, z, y_lo, core, zc, xy = place()
+    peers = []
+    for step in ZC_STEPS:
+        peer = (zc + step) & (GROUP - 1)
+        peers.append((peer, (row, (peer >> 1) * 4 + y_lo * 2 + (peer & 1))))
+    return peers
+
+
+def xy_peers():
+    row, z, y_lo, core, zc, xy = place()
+    rows = [((row >> 1) + step) & 3 for step in range(4)]
+    columns = [((row & 1) * 2 + y_lo + step) & 3 for step in range(4)]
+    peers = []
+    for step in XY_STEPS:
+        x, y = rows[step[0]], columns[step[1]]
+        peers.append((x * 4 + y, (x * 2 + (y >> 1), z * 4 + (y & 1) * 2 + core)))
+    return peers
+
+
 def distances(tile, centre):
     x, y = ((tile >> 2) - (centre >> 2)) & 3, ((tile & 3) - (centre & 3)) & 3
     return jnp.minimum(x, 4 - x) + jnp.minimum(y, 4 - y), x * 4 + y
@@ -56,9 +63,8 @@
 
 def greet():
     barrier = pltpu.get_barrier_semaphore()
-    for peer, steps in ((zc_peer, ZC_STEPS), (xy_peer, XY_STEPS)):
-        for step in steps:
-            pl.semaphore_signal(barrier, inc=1, device_id=peer(step)[1], device_id_type=MESH)
+    for peer, device in zc_peers() + xy_peers():
+        pl.semaphore_signal(barrier, inc=1, device_id=device, device_id_type=MESH)
 
 
 def await_greetings():
@@ -195,10 +201,9 @@
         total = jnp.where(lane == zc * ACT + slot, value, total)
     mine[...] = total
     await_greetings()
-    for step in ZC_STEPS:
-        peer, device = zc_peer(step)
+    for at, (peer, device) in enumerate(zc_peers()):
         pltpu.make_async_remote_copy(
-            src_ref=mine, dst_ref=near.at[step - 1],
+            src_ref=mine, dst_ref=near.at[at],
             send_sem=send_sem.at[0], recv_sem=recv_sem.at[0],
             device_id=device, device_id_type=MESH).start()
 
@@ -211,8 +216,7 @@
     for step in range(1, GROUP):
         total = total + near[step - 1]
     all_ref[pl.ds(xy, 1)] = total[None]
-    for step in XY_STEPS:
-        peer, device = xy_peer(step)
+    for peer, device in xy_peers():
         pltpu.make_async_remote_copy(
             src_ref=all_ref.at[xy], dst_ref=all_ref.at[xy],
             send_sem=send_sem.at[1], recv_sem=recv_sem.at[1],
@@ -272,9 +276,12 @@
     row_id = lax.broadcasted_iota(jnp.int32, (8, LANES), 0)
     for at in range(tiles):
         cols = pl.ds(at * LANES, LANES)
-        target = jnp.where((row_id == 3) | (row_id == 7), 0.0, packed[at])
-        target_ref[:, cols] = target
-        near_ref[:, cols], along_ref[:, cols] = target_features(target)
+        target_ref[:, cols] = jnp.where((row_id == 3) | (row_id == 7), 0.0, packed[at])
+
+    def weigh(cols):
+        near_ref[:, cols], along_ref[:, cols] = target_features(target_ref[:, cols])
+
+    weigh(pl.ds(0, BLOCK))
     sub = lax.broadcasted_iota(jnp.int32, (8, BLOCK), 0)
 
     def block(index, carry):
@@ -293,6 +300,7 @@
         target = target_ref[:, cols]
         by_w, by_u = [total - target * total[3:4, :] for total in sums]
         force_ref[:, cols] = by_w - 3.0 * jnp.where(sub >= 4, pltpu.roll(by_u, 4, 0), 0.0)
+        weigh(pl.ds(pl.multiple_of(lax.rem(index + 1, blocks) * BLOCK, BLOCK), BLOCK))
         return carry
 
     def unpack(peer, done):
@@ -309,7 +317,7 @@
             device_id=device, device_id_type=MESH).start()
 
     row, z, y_lo, core, zc, xy = place()
-    peers = [xy_peer(step) for step in XY_STEPS]
+    peers = xy_peers()
 
     def send_far():
         for peer, device in peers[:FAR]:
@@ -335,10 +343,9 @@
     for step in range(1, GROUP):
         total = total + first[step - 1]
     summed[...] = total
-    for step in ZC_STEPS:
-        peer, device = zc_peer(step)
+    for at, (peer, device) in enumerate(zc_peers()):
         pltpu.make_async_remote_copy(
-            src_ref=summed, dst_ref=second.at[step - 1],
+            src_ref=summed, dst_ref=second.at[at],
             send_sem=send_sem.at[1], recv_sem=recv_sem.at[1],
             device_id=device, device_id_type=MESH).start()
     wait_bytes(second, recv_sem.at[1])

time: 42.7 us -> 42.4 us (level)
  no operation moved by 1% of the time
where the time goes in v8:
time: 42.4 us; the launch traced here: 42.3 us
  Pallas kernels  40.3 us (95%)
  between operations  1.93 us (5%)
    pallas_call x1, Pallas kernels, local(): pl.pallas_call(gather_kernel, out_shape=(jax.ShapeDtypeStruct((STARS, LAN...  20.4 us
    pallas_call x1, Pallas kernels, local(): lax.switch(choice[0], branches, active_count, features, moments, everyone...  19.4 us

profile of v8, /device:TPU:1, one launch (start us, length us, event | category | flops | bytes accessed | tf_op | source)
XLA Modules:
  0.0 42.3 jit_solution(11759729117505648375)
XLA Ops:
  1.3 20.4 %gather_targets.1 = (bf16[4096,128]{1,0:T(8,128)(2,1)S(1)}, bf16[32,4096]{1,0:T(8,128)(2,1)S(1)}, f32[16,8,128]{2,1,0:T(8,128)S(1)}, f32[2,16,128]{2,1,0:T(8,128)S(1)}, s32[1]{0:T(128)}) custom-call(s32[8]{0:T(128)} %index_ref.1, s32[1]{0:T(128)S(6)} %copy.13.count_ref, f32[3,4096]{1,0:T(4,128)} %pos_hbm.1, f32[3,4096]{1,0:T(4,128)} %vel_hbm.1, ...), custom_call_target="tpu_custom_call" | custom-call | tf_op jit(solution)/shard_map/gather_targets/pallas_call | solution.py:371
  22.3 19.4 %conditional.1 = (f32[8,128]{1,0:T(8,128)S(1)}) conditional(s32[]{:T(128)} %bitcast.2, (s32[1]{0:T(128)}, bf16[4096,128]{1,0:T(8,128)(2,1)S(1)}, bf16[32,4096]{1,0:T(8,128)(2,1)S(1)}, f32[16,8,128]{2,1,0:T(8,128)S(1)}, f32[2,16,128]{2,1,0:T(8,128)S(1)}) %tuple.16, (s32[1]{0:T(128)}, bf16[4096,128]{1,0:T(8,128)(2,1)S(1)}, ...), branch_computations={%region_0.0_spmd, %region_1.0_spmd, %region_2.0_spmd} | conditional | bytes 8 | solution.py:421
  22.3 19.4 %forces_3.1 = f32[8,128]{1,0:T(8,128)S(1)} custom-call(s32[1]{0:T(128)} %get-tuple-element.14.count_ref, bf16[4096,128]{1,0:T(8,128)(2,1)S(1)} %get-tuple-element.24.feature_ref, bf16[32,4096]{1,0:T(8,128)(2,1)S(1)} %get-tuple-element.36.moment_ref, f32[16,8,128]{2,1,0:T(8,128)S(1)} %get-tuple-element.37.all_ref, f32[2,16,128]{2,1,0:T(8,128)S(1)} %get-tuple-element.38.rank_ref), custom_call_target="tpu_custom_call" | custom-call | tf_op jit(solution)/shard_map/cond/branch_0_fun/forces_3/pallas_call | solution.py:421
  41.7 0.6 %finish.1 = (f32[3,8]{1,0:T(4,128)}, f32[3,8]{1,0:T(4,128)}) custom-call(f32[8,128]{1,0:T(8,128)S(1)} %get-tuple-element.61.force_ref), custom_call_target="tpu_custom_call" | custom-call | tf_op jit(solution)/shard_map/finish/pallas_call | solution.py:422

commit v9 on v8

--- a/solution.py
+++ b/solution.py
@@ -243,7 +243,7 @@
     rank_ref[0] = jnp.where(alive > 0.0, lead - LANES * jnp.floor(lead * (1.0 / LANES)), -1.0)
     spot = lax.broadcasted_iota(jnp.int32, (GROUP, LANES), 1).astype(F32)
     rank_ref[1] = jnp.floor(ahead * (1.0 / LANES)) + jnp.where(spot < first, 1.0, 0.0)
-    live = jnp.max(ahead + sums, axis=0, keepdims=True)
+    live = jnp.max(ahead + sums, axis=0, keepdims=True) - jnp.min(sums, axis=0, keepdims=True)
     far = jnp.max(far, axis=0, keepdims=True)
     choice = jnp.full((1, LANES), len(SIZES) - 1.0, F32)
     for at in reversed(range(len(SIZES) - 1)):
@@ -259,6 +259,23 @@
 
 def joined(rows):
     return rows[0:8] + rows[8:16] + rows[16:24]
+
+
+def pair_weights(r2, dot):
+    inv = lax.rsqrt(r2)
+    inv2 = inv * inv
+    w = inv * inv2
+    out = []
+    for value in (w, (w * inv2) * dot):
+        high = value.astype(BF16)
+        out.append((high, (value - high.astype(F32)).astype(BF16)))
+    return out
+
+
+def force_of(by_w, by_u, target):
+    sub = lax.broadcasted_iota(jnp.int32, target.shape, 0)
+    by_w, by_u = by_w - target * by_w[3:4, :], by_u - target * by_u[3:4, :]
+    return by_w - 3.0 * jnp.where(sub >= 4, pltpu.roll(by_u, 4, 0), 0.0)
 
 
 def force_kernel(blocks, early, count_ref, feature_ref, moment_ref, all_ref, rank_ref, out_ref,
@@ -282,24 +299,13 @@
         near_ref[:, cols], along_ref[:, cols] = target_features(target_ref[:, cols])
 
     weigh(pl.ds(0, BLOCK))
-    sub = lax.broadcasted_iota(jnp.int32, (8, BLOCK), 0)
 
     def block(index, carry):
         cols = pl.ds(pl.multiple_of(index * BLOCK, BLOCK), BLOCK)
         r2 = mm(feature_ref[...], near_ref[:, cols])
         dot = mm(feature_ref[...], along_ref[:, cols])
-        inv = lax.rsqrt(r2)
-        inv2 = inv * inv
-        w = inv * inv2
-        u = (w * inv2) * dot
-        sums = []
-        for value in (w, u):
-            high = value.astype(BF16)
-            low = (value - high.astype(F32)).astype(BF16)
-            sums.append(joined(mm(moment_ref[...], high) + mm(moment_ref[...], low)))
-        target = target_ref[:, cols]
-        by_w, by_u = [total - target * total[3:4, :] for total in sums]
-        force_ref[:, cols] = by_w - 3.0 * jnp.where(sub >= 4, pltpu.roll(by_u, 4, 0), 0.0)
+        sums = [joined(mm(moment_ref[...], high) + mm(moment_ref[...], low)) for high, low in pair_weights(r2, dot)]
+        force_ref[:, cols] = force_of(*sums, target_ref[:, cols])
         weigh(pl.ds(pl.multiple_of(lax.rem(index + 1, blocks) * BLOCK, BLOCK), BLOCK))
         return carry
 
@@ -333,12 +339,16 @@
     lax.fori_loop(0, blocks, step, 0)
     if early == blocks:
         send_far()
-    for peer, device in peers[FAR:]:
-        unpack(peer, blocks)
     for at in range(FAR, GROUP - 1):
+        unpack(peers[at][0], blocks)
         send(at, *peers[at])
-    unpack(xy, blocks)
-    total = part_ref[xy]
+    target = jnp.where((row_id == 3) | (row_id == 7), 0.0, all_ref[xy])
+    both = mm(feature_ref[...], jnp.concatenate(target_features(target), 1))
+    sums = []
+    for high, low in pair_weights(both[:, :LANES], both[:, LANES:]):
+        halves = mm(moment_ref[...], jnp.concatenate([high, low], 1))
+        sums.append(joined(halves[:, :LANES] + halves[:, LANES:]))
+    total = force_of(*sums, target)
     wait_bytes(first, recv_sem.at[0])
     for step in range(1, GROUP):
         total = total + first[step - 1]

time: 42.4 us -> 43.2 us (1.019)
  Pallas kernels: 40.3 us -> 40.8 us
    pallas_call x1, Pallas kernels: 19.4 us -> 19.9 us  [local(): lax.switch(choice[0], branches, active_count, features, moments, everyone...]
where the time goes in v9:
time: 43.2 us; the launch traced here: 43 us
  Pallas kernels  40.8 us (94%)
  between operations  1.93 us (4%)
    pallas_call x1, Pallas kernels, local(): pl.pallas_call(gather_kernel, out_shape=(jax.ShapeDtypeStruct((STARS, LAN...  20.4 us
    pallas_call x1, Pallas kernels, local(): lax.switch(choice[0], branches, active_count, features, moments, everyone...  19.9 us

profile of v9, /device:TPU:1, one launch (start us, length us, event | category | flops | bytes accessed | tf_op | source)
XLA Modules:
  0.0 43.0 jit_solution(5980551231061432516)
XLA Ops:
  1.3 20.4 %gather_targets.1 = (bf16[4096,128]{1,0:T(8,128)(2,1)S(1)}, bf16[32,4096]{1,0:T(8,128)(2,1)S(1)}, f32[16,8,128]{2,1,0:T(8,128)S(1)}, f32[2,16,128]{2,1,0:T(8,128)S(1)}, s32[1]{0:T(128)}) custom-call(s32[8]{0:T(128)} %index_ref.1, s32[1]{0:T(128)S(6)} %copy.13.count_ref, f32[3,4096]{1,0:T(4,128)} %pos_hbm.1, f32[3,4096]{1,0:T(4,128)} %vel_hbm.1, ...), custom_call_target="tpu_custom_call" | custom-call | tf_op jit(solution)/shard_map/gather_targets/pallas_call | solution.py:381
  22.3 20.1 %conditional.1 = (f32[8,128]{1,0:T(8,128)S(1)}) conditional(s32[]{:T(128)} %bitcast.2, (s32[1]{0:T(128)}, bf16[4096,128]{1,0:T(8,128)(2,1)S(1)}, bf16[32,4096]{1,0:T(8,128)(2,1)S(1)}, f32[16,8,128]{2,1,0:T(8,128)S(1)}, f32[2,16,128]{2,1,0:T(8,128)S(1)}) %tuple.16, (s32[1]{0:T(128)}, bf16[4096,128]{1,0:T(8,128)(2,1)S(1)}, ...), branch_computations={%region_0.0_spmd, %region_1.0_spmd, %region_2.0_spmd} | conditional | bytes 8 | solution.py:431
  22.3 19.9 %forces_3.1 = f32[8,128]{1,0:T(8,128)S(1)} custom-call(s32[1]{0:T(128)} %get-tuple-element.14.count_ref, bf16[4096,128]{1,0:T(8,128)(2,1)S(1)} %get-tuple-element.24.feature_ref, bf16[32,4096]{1,0:T(8,128)(2,1)S(1)} %get-tuple-element.36.moment_ref, f32[16,8,128]{2,1,0:T(8,128)S(1)} %get-tuple-element.37.all_ref, f32[2,16,128]{2,1,0:T(8,128)S(1)} %get-tuple-element.38.rank_ref), custom_call_target="tpu_custom_call" | custom-call | tf_op jit(solution)/shard_map/cond/branch_0_fun/forces_3/pallas_call | solution.py:431
  42.4 0.6 %finish.1 = (f32[3,8]{1,0:T(4,128)}, f32[3,8]{1,0:T(4,128)}) custom-call(f32[8,128]{1,0:T(8,128)S(1)} %get-tuple-element.61.force_ref), custom_call_target="tpu_custom_call" | custom-call | tf_op jit(solution)/shard_map/finish/pallas_call | solution.py:432

commit v10 on v9

--- a/solution.py
+++ b/solution.py
@@ -16,7 +16,7 @@
 STARS = 4096
 TILES = STARS // LANES
 BLOCK = 256
-SIZES = ((3, 2), (4, 2), (8, 8))
+SIZES = ((3, 2, False), (3, 2, True), (4, 2, False), (8, 8, False))
 
 
 def ring(size, step):
@@ -243,12 +243,14 @@
     rank_ref[0] = jnp.where(alive > 0.0, lead - LANES * jnp.floor(lead * (1.0 / LANES)), -1.0)
     spot = lax.broadcasted_iota(jnp.int32, (GROUP, LANES), 1).astype(F32)
     rank_ref[1] = jnp.floor(ahead * (1.0 / LANES)) + jnp.where(spot < first, 1.0, 0.0)
-    live = jnp.max(ahead + sums, axis=0, keepdims=True) - jnp.min(sums, axis=0, keepdims=True)
+    live = jnp.max(ahead + sums, axis=0, keepdims=True)
+    others = live - jnp.min(sums, axis=0, keepdims=True)
     far = jnp.max(far, axis=0, keepdims=True)
     choice = jnp.full((1, LANES), len(SIZES) - 1.0, F32)
     for at in reversed(range(len(SIZES) - 1)):
-        blocks, early = SIZES[at]
-        choice = jnp.where((live <= blocks * BLOCK) & (far <= early * BLOCK), float(at), choice)
+        blocks, early, apart = SIZES[at]
+        need = others if apart else live
+        choice = jnp.where((need <= blocks * BLOCK) & (far <= early * BLOCK), float(at), choice)
     choice_ref[0] = choice[0, 0].astype(jnp.int32)
     wait_bytes(near, send_sem.at[1])
 
@@ -278,7 +280,18 @@
     return by_w - 3.0 * jnp.where(sub >= 4, pltpu.roll(by_u, 4, 0), 0.0)
 
 
-def force_kernel(blocks, early, count_ref, feature_ref, moment_ref, all_ref, rank_ref, out_ref,
+def force_apart(group, feature_ref, moment_ref):
+    sub = lax.broadcasted_iota(jnp.int32, group.shape, 0)
+    target = jnp.where((sub == 3) | (sub == 7), 0.0, group)
+    both = mm(feature_ref[...], jnp.concatenate(target_features(target), 1))
+    sums = []
+    for high, low in pair_weights(both[:, :LANES], both[:, LANES:]):
+        halves = mm(moment_ref[...], jnp.concatenate([high, low], 1))
+        sums.append(joined(halves[:, :LANES] + halves[:, LANES:]))
+    return force_of(*sums, target)
+
+
+def force_kernel(blocks, early, apart, count_ref, feature_ref, moment_ref, all_ref, rank_ref, out_ref,
                  part_ref, hot, near_ref, along_ref, target_ref, force_ref,
                  first, second, summed, send_sem, recv_sem):
     greet()
@@ -342,13 +355,11 @@
     for at in range(FAR, GROUP - 1):
         unpack(peers[at][0], blocks)
         send(at, *peers[at])
-    target = jnp.where((row_id == 3) | (row_id == 7), 0.0, all_ref[xy])
-    both = mm(feature_ref[...], jnp.concatenate(target_features(target), 1))
-    sums = []
-    for high, low in pair_weights(both[:, :LANES], both[:, LANES:]):
-        halves = mm(moment_ref[...], jnp.concatenate([high, low], 1))
-        sums.append(joined(halves[:, :LANES] + halves[:, LANES:]))
-    total = force_of(*sums, target)
+    if apart:
+        total = force_apart(all_ref[xy], feature_ref, moment_ref)
+    else:
+        unpack(xy, blocks)
+        total = part_ref[xy]
     wait_bytes(first, recv_sem.at[0])
     for step in range(1, GROUP):
         total = total + first[step - 1]
@@ -424,7 +435,7 @@
             ],
             compiler_params=pltpu.CompilerParams(
                 collective_id=1 + at, has_side_effects=True, vmem_limit_bytes=24 * 2**20),
-            name="forces_%d" % SIZES[at][0],
+            name="forces_%d%s" % (SIZES[at][0], "_apart" if SIZES[at][2] else ""),
         )
 
     branches = [forces(at) for at in range(len(SIZES))]

time: 43.2 us -> 43.2 us (level)
  no operation moved by 1% of the time
where the time goes in v10:
time: 43.2 us; the launch traced here: 43 us
  Pallas kernels  40.8 us (94%)
  between operations  1.93 us (4%)
    pallas_call x1, Pallas kernels, local(): pl.pallas_call(gather_kernel, out_shape=(jax.ShapeDtypeStruct((STARS, LAN...  20.4 us
    pallas_call x1, Pallas kernels, local(): lax.switch(choice[0], branches, active_count, features, moments, everyone...  19.9 us

profile of v10, /device:TPU:1, one launch (start us, length us, event | category | flops | bytes accessed | tf_op | source)
XLA Modules:
  0.0 43.0 jit_solution(12422844949648744122)
XLA Ops:
  1.3 20.4 %gather_targets.1 = (bf16[4096,128]{1,0:T(8,128)(2,1)S(1)}, bf16[32,4096]{1,0:T(8,128)(2,1)S(1)}, f32[16,8,128]{2,1,0:T(8,128)S(1)}, f32[2,16,128]{2,1,0:T(8,128)S(1)}, s32[1]{0:T(128)}) custom-call(s32[8]{0:T(128)} %index_ref.1, s32[1]{0:T(128)S(6)} %copy.14.count_ref, f32[3,4096]{1,0:T(4,128)} %pos_hbm.1, f32[3,4096]{1,0:T(4,128)} %vel_hbm.1, ...), custom_call_target="tpu_custom_call" | custom-call | tf_op jit(solution)/shard_map/gather_targets/pallas_call | solution.py:392
  22.3 20.1 %conditional.1 = (f32[8,128]{1,0:T(8,128)S(1)}) conditional(s32[]{:T(128)} %bitcast.2, (s32[1]{0:T(128)}, bf16[4096,128]{1,0:T(8,128)(2,1)S(1)}, bf16[32,4096]{1,0:T(8,128)(2,1)S(1)}, f32[16,8,128]{2,1,0:T(8,128)S(1)}, f32[2,16,128]{2,1,0:T(8,128)S(1)}) %tuple.19, (s32[1]{0:T(128)}, bf16[4096,128]{1,0:T(8,128)(2,1)S(1)}, ...), branch_computations={%region_0.0_spmd, %region_1.0_spmd, %region_2.0_spmd, %region_3.0_... | conditional | bytes 8 | solution.py:442
  22.3 19.9 %forces_3.1 = f32[8,128]{1,0:T(8,128)S(1)} custom-call(s32[1]{0:T(128)} %get-tuple-element.24.count_ref, bf16[4096,128]{1,0:T(8,128)(2,1)S(1)} %get-tuple-element.40.feature_ref, bf16[32,4096]{1,0:T(8,128)(2,1)S(1)} %get-tuple-element.41.moment_ref, f32[16,8,128]{2,1,0:T(8,128)S(1)} %get-tuple-element.48.all_ref, f32[2,16,128]{2,1,0:T(8,128)S(1)} %get-tuple-element.49.rank_ref), custom_call_target="tpu_custom_call" | custom-call | tf_op jit(solution)/shard_map/cond/branch_0_fun/forces_3/pallas_call | solution.py:442
  42.4 0.6 %finish.1 = (f32[3,8]{1,0:T(4,128)}, f32[3,8]{1,0:T(4,128)}) custom-call(f32[8,128]{1,0:T(8,128)S(1)} %get-tuple-element.77.force_ref), custom_call_target="tpu_custom_call" | custom-call | tf_op jit(solution)/shard_map/finish/pallas_call | solution.py:443

commit v11 on v10

--- a/solution.py
+++ b/solution.py
@@ -259,8 +259,12 @@
     return jnp.concatenate(list(pieces(group)) + [jnp.zeros_like(group)], 0).astype(BF16)
 
 
+def halved(rows):
+    return rows[0:8] + rows[8:16]
+
+
 def joined(rows):
-    return rows[0:8] + rows[8:16] + rows[16:24]
+    return halved(rows) + rows[16:24]
 
 
 def pair_weights(r2, dot):
@@ -317,7 +321,8 @@
         cols = pl.ds(pl.multiple_of(index * BLOCK, BLOCK), BLOCK)
         r2 = mm(feature_ref[...], near_ref[:, cols])
         dot = mm(feature_ref[...], along_ref[:, cols])
-        sums = [joined(mm(moment_ref[...], high) + mm(moment_ref[...], low)) for high, low in pair_weights(r2, dot)]
+        sums = [halved(mm(moment_ref[0:16, :], low)) + joined(mm(moment_ref[...], high))
+                for high, low in pair_weights(r2, dot)]
         force_ref[:, cols] = force_of(*sums, target_ref[:, cols])
         weigh(pl.ds(pl.multiple_of(lax.rem(index + 1, blocks) * BLOCK, BLOCK), BLOCK))
         return carry

time: 43.2 us -> 41.9 us (0.970)
  Pallas kernels: 40.8 us -> 39.5 us
    pallas_call x1, Pallas kernels: 19.9 us -> 18.6 us  [local(): lax.switch(choice[0], branches, active_count, features, moments, everyone...]
where the time goes in v11:
time: 41.9 us; the launch traced here: 41.7 us
  Pallas kernels  39.5 us (94%)
  between operations  1.93 us (5%)
    pallas_call x1, Pallas kernels, local(): pl.pallas_call(gather_kernel, out_shape=(jax.ShapeDtypeStruct((STARS, LAN...  20.4 us
    pallas_call x1, Pallas kernels, local(): lax.switch(choice[0], branches, active_count, features, moments, everyone...  18.6 us

profile of v11, /device:TPU:1, one launch (start us, length us, event | category | flops | bytes accessed | tf_op | source)
XLA Modules:
  0.0 41.7 jit_solution(9890841378893225403)
XLA Ops:
  1.3 20.4 %gather_targets.1 = (bf16[4096,128]{1,0:T(8,128)(2,1)S(1)}, bf16[32,4096]{1,0:T(8,128)(2,1)S(1)}, f32[16,8,128]{2,1,0:T(8,128)S(1)}, f32[2,16,128]{2,1,0:T(8,128)S(1)}, s32[1]{0:T(128)}) custom-call(s32[8]{0:T(128)} %index_ref.1, s32[1]{0:T(128)S(6)} %copy.14.count_ref, f32[3,4096]{1,0:T(4,128)} %pos_hbm.1, f32[3,4096]{1,0:T(4,128)} %vel_hbm.1, ...), custom_call_target="tpu_custom_call" | custom-call | tf_op jit(solution)/shard_map/gather_targets/pallas_call | solution.py:397
  22.3 18.8 %conditional.1 = (f32[8,128]{1,0:T(8,128)S(1)}) conditional(s32[]{:T(128)} %bitcast.2, (s32[1]{0:T(128)}, bf16[4096,128]{1,0:T(8,128)(2,1)S(1)}, bf16[32,4096]{1,0:T(8,128)(2,1)S(1)}, f32[16,8,128]{2,1,0:T(8,128)S(1)}, f32[2,16,128]{2,1,0:T(8,128)S(1)}) %tuple.19, (s32[1]{0:T(128)}, bf16[4096,128]{1,0:T(8,128)(2,1)S(1)}, ...), branch_computations={%region_0.0_spmd, %region_1.0_spmd, %region_2.0_spmd, %region_3.0_... | conditional | bytes 8 | solution.py:447
  22.3 18.6 %forces_3_apart.1 = f32[8,128]{1,0:T(8,128)S(1)} custom-call(s32[1]{0:T(128)} %get-tuple-element.50.count_ref, bf16[4096,128]{1,0:T(8,128)(2,1)S(1)} %get-tuple-element.51.feature_ref, bf16[32,4096]{1,0:T(8,128)(2,1)S(1)} %get-tuple-element.52.moment_ref, f32[16,8,128]{2,1,0:T(8,128)S(1)} %get-tuple-element.53.all_ref, ...), custom_call_target="tpu_custom_call" | custom-call | tf_op jit(solution)/shard_map/cond/branch_1_fun/forces_3_apart/pallas_call | solution.py:447
  41.1 0.6 %finish.1 = (f32[3,8]{1,0:T(4,128)}, f32[3,8]{1,0:T(4,128)}) custom-call(f32[8,128]{1,0:T(8,128)S(1)} %get-tuple-element.77.force_ref), custom_call_target="tpu_custom_call" | custom-call | tf_op jit(solution)/shard_map/finish/pallas_call | solution.py:448

commit v12 on v11

--- a/solution.py
+++ b/solution.py
@@ -318,13 +318,17 @@
     weigh(pl.ds(0, BLOCK))
 
     def block(index, carry):
-        cols = pl.ds(pl.multiple_of(index * BLOCK, BLOCK), BLOCK)
+        lead = index * BLOCK
+        cols = pl.ds(lead if isinstance(index, int) else pl.multiple_of(lead, BLOCK), BLOCK)
         r2 = mm(feature_ref[...], near_ref[:, cols])
         dot = mm(feature_ref[...], along_ref[:, cols])
         sums = [halved(mm(moment_ref[0:16, :], low)) + joined(mm(moment_ref[...], high))
                 for high, low in pair_weights(r2, dot)]
         force_ref[:, cols] = force_of(*sums, target_ref[:, cols])
-        weigh(pl.ds(pl.multiple_of(lax.rem(index + 1, blocks) * BLOCK, BLOCK), BLOCK))
+        if not isinstance(index, int):
+            weigh(pl.ds(pl.multiple_of(lax.rem(index + 1, blocks) * BLOCK, BLOCK), BLOCK))
+        elif index + 1 < blocks:
+            weigh(pl.ds((index + 1) * BLOCK, BLOCK))
         return carry
 
     def unpack(peer, done):
@@ -354,7 +358,13 @@
         pl.when(index == early)(send_far)
         return block(index, carry)
 
-    lax.fori_loop(0, blocks, step, 0)
+    if blocks == 3:
+        for index in range(blocks):
+            if index == early:
+                send_far()
+            block(index, 0)
+    else:
+        lax.fori_loop(0, blocks, step, 0)
     if early == blocks:
         send_far()
     for at in range(FAR, GROUP - 1):

time: 41.9 us -> 42 us (level)
  no operation moved by 1% of the time
where the time goes in v12:
time: 42 us; the launch traced here: 41.8 us
  Pallas kernels  39.5 us (94%)
  between operations  1.93 us (5%)
  loops' own time  0.43 us (1%)
    pallas_call x1, Pallas kernels, local(): pl.pallas_call(gather_kernel, out_shape=(jax.ShapeDtypeStruct((STARS, LAN...  20.4 us
    pallas_call x1, Pallas kernels, local(): lax.switch(choice[0], branches, active_count, features, moments, everyone...  18.5 us

profile of v12, /device:TPU:1, one launch (start us, length us, event | category | flops | bytes accessed | tf_op | source)
XLA Modules:
  0.0 41.8 jit_solution(10956826848125966602)
XLA Ops:
  1.3 20.4 %gather_targets.1 = (bf16[4096,128]{1,0:T(8,128)(2,1)S(1)}, bf16[32,4096]{1,0:T(8,128)(2,1)S(1)}, f32[16,8,128]{2,1,0:T(8,128)S(1)}, f32[2,16,128]{2,1,0:T(8,128)S(1)}, s32[1]{0:T(128)}) custom-call(s32[8]{0:T(128)} %index_ref.1, s32[1]{0:T(128)S(6)} %copy.14.count_ref, f32[3,4096]{1,0:T(4,128)} %pos_hbm.1, f32[3,4096]{1,0:T(4,128)} %vel_hbm.1, ...), custom_call_target="tpu_custom_call" | custom-call | tf_op jit(solution)/shard_map/gather_targets/pallas_call | solution.py:407
  22.3 18.9 %conditional.1 = (f32[8,128]{1,0:T(8,128)S(1)}) conditional(s32[]{:T(128)} %bitcast.2, (s32[1]{0:T(128)}, bf16[4096,128]{1,0:T(8,128)(2,1)S(1)}, bf16[32,4096]{1,0:T(8,128)(2,1)S(1)}, f32[16,8,128]{2,1,0:T(8,128)S(1)}, f32[2,16,128]{2,1,0:T(8,128)S(1)}) %tuple.19, (s32[1]{0:T(128)}, bf16[4096,128]{1,0:T(8,128)(2,1)S(1)}, ...), branch_computations={%region_0.0_spmd, %region_1.0_spmd, %region_2.0_spmd, %region_3.0_... | conditional | bytes 8 | solution.py:457
  22.3 18.5 %forces_3.1 = f32[8,128]{1,0:T(8,128)S(1)} custom-call(s32[1]{0:T(128)} %get-tuple-element.24.count_ref, bf16[4096,128]{1,0:T(8,128)(2,1)S(1)} %get-tuple-element.40.feature_ref, bf16[32,4096]{1,0:T(8,128)(2,1)S(1)} %get-tuple-element.41.moment_ref, f32[16,8,128]{2,1,0:T(8,128)S(1)} %get-tuple-element.48.all_ref, f32[2,16,128]{2,1,0:T(8,128)S(1)} %get-tuple-element.49.rank_ref), custom_call_target="tpu_custom_call" | custom-call | tf_op jit(solution)/shard_map/cond/branch_0_fun/forces_3/pallas_call | solution.py:457
  41.2 0.6 %finish.1 = (f32[3,8]{1,0:T(4,128)}, f32[3,8]{1,0:T(4,128)}) custom-call(f32[8,128]{1,0:T(8,128)S(1)} %get-tuple-element.77.force_ref), custom_call_target="tpu_custom_call" | custom-call | tf_op jit(solution)/shard_map/finish/pallas_call | solution.py:458
